TPU v7x, 128 devices: a whole 4x4x4 slice. The times are simulated.
128 devices in a mesh: rep: 2 (over z_lo), shard: 64 (over y, x, z_hi, core).
Axes of the slice: x: 4, y: 4, z: 4 (z_hi: 2, z_lo: 2; z = z_hi * 2 + z_lo), core: 2. Of those that a mesh axis runs over, the one named last changes fastest.
Arguments:
- tokens: bfloat16 [32768, 1024], P(('rep', 'shard')), may hold values from -6 to 6
- lengths: int32 [2], replicated, may hold values from 4096 to 16384, as said below
- norm1_gain: bfloat16 [1024], P('shard'), may hold values from 0.099609375 to 1.8984375
- in_proj: bfloat16 [1024, 3072], P('shard'), may hold values from -0.1875 to 0.1875
- conv_weight: bfloat16 [3, 1024], P(None, 'shard'), may hold values from -3.5 to 3.5
- out_proj: bfloat16 [1024, 1024], P('shard'), may hold values from -0.1875 to 0.1875
- norm2_gain: bfloat16 [1024], P('shard'), may hold values from 0.099609375 to 1.8984375
- w_gate: bfloat16 [1024, 4608], P('shard'), may hold values from -0.1875 to 0.1875
- w_up: bfloat16 [1024, 4608], P('shard'), may hold values from -0.1875 to 0.1875
- w_down: bfloat16 [4608, 1024], P('shard'), may hold values from -0.09375 to 0.09375
- cotangent: bfloat16 [32768, 1024], P(('rep', 'shard')), may hold values from -6 to 6
Outputs:
- mixed: bfloat16 [32768, 1024], P(('rep', 'shard'))
- d_tokens: float32 [32768, 1024], P(('rep', 'shard'))
- d_norm1_gain: float32 [1024], P('shard')
- d_in_proj: float32 [1024, 3072], P('shard')
- d_conv_weight: float32 [3, 1024], P(None, 'shard')
- d_out_proj: float32 [1024, 1024], P('shard')
- d_norm2_gain: float32 [1024], P('shard')
- d_w_gate: float32 [1024, 4608], P('shard')
- d_w_up: float32 [1024, 4608], P('shard')
- d_w_down: float32 [4608, 1024], P('shard')
Inputs may be any that keep to these rules, and one draw needn't show every extreme that they name: `lengths`: each slot holds 4096 to 16384 valid tokens at its start; at least one slot is full.
All inputs are finite; a program needn't handle non-finite values.
Results may differ from a plain program's by a relative error of at most 0.019.
Values may be sent and summed in bfloat16 or wider, within the bound.
A program may use at most 192 MiB of HBM per device.

v0:
```python
import jax
import jax.numpy as jnp
from jax import lax
from jax.sharding import PartitionSpec as P

EPS = 1e-05


def from_behind(value, axis, steps):
    count = lax.axis_size(axis)
    initial, last = (max(0, -steps), min(count, count - steps))
    return lax.ppermute(value, axis, [(source, source + steps) for source in range(initial, last)])


def norm_rows(rows, gain):
    scale = lax.rsqrt(jnp.mean(rows * rows, axis=1, keepdims=True) + EPS)
    return (scale, rows * scale * gain)


def norm_back(rows, scale, gain, grad_norm):
    gain_grad = jnp.sum(grad_norm * rows * scale, axis=0)
    weighted = grad_norm * gain
    inner = jnp.mean(weighted * rows, axis=1, keepdims=True)
    return (scale * weighted - rows * (scale * scale * scale) * inner, gain_grad)


def weight_grad(left, right):
    return lax.dot_general(
        left, right, (((0,), (0,)), ((), ())), preferred_element_type=jnp.float32
    )


def input_grad(grad, weight):
    return lax.dot_general(
        grad, weight, (((1,), (1,)), ((), ())), preferred_element_type=jnp.float32
    )


def body(
    tokens,
    lengths,
    norm1_gain,
    in_proj,
    conv_weight,
    out_proj,
    norm2_gain,
    w_gate,
    w_up,
    w_down,
    cotangent,
):
    rows, width = tokens.shape
    place = lax.axis_index("shard")
    slot = lax.axis_index("rep")
    slot_ids = jnp.arange(lengths.shape[0], dtype=jnp.int32)
    length = jnp.sum(jnp.where(slot_ids == slot, lengths, 0))
    valid = jnp.clip(length - place * rows, 0, rows)
    keep = (jnp.arange(rows, dtype=jnp.int32) < valid).astype(jnp.float32)[:, None]
    inside = (place > 0).astype(jnp.float32)
    full = (
        lax.all_gather(norm1_gain, "shard", axis=0, tiled=True),
        lax.all_gather(in_proj, "shard", axis=0, tiled=True),
        lax.all_gather(conv_weight, "shard", axis=1, tiled=True),
        lax.all_gather(out_proj, "shard", axis=0, tiled=True),
        lax.all_gather(norm2_gain, "shard", axis=0, tiled=True),
        lax.all_gather(w_gate, "shard", axis=0, tiled=True),
        lax.all_gather(w_up, "shard", axis=0, tiled=True),
        lax.all_gather(w_down, "shard", axis=0, tiled=True),
    )
    source = tokens.astype(jnp.float32)
    gain_one = full[0].astype(jnp.float32)
    taps = full[2].astype(jnp.float32)
    gain_two = full[4].astype(jnp.float32)
    scale_one, normed_f = norm_rows(source, gain_one)
    normed = normed_f.astype(jnp.bfloat16)
    bcx = jnp.dot(normed, full[1], preferred_element_type=jnp.float32)
    b_part = bcx[:, :width]
    c_part = bcx[:, width : 2 * width]
    x_part = bcx[:, 2 * width :]
    product = (b_part * x_part).astype(jnp.bfloat16)
    edge = from_behind(product[rows - 2 :], "shard", 1)
    extended = jnp.concatenate(
        [edge.astype(jnp.float32) * inside, product.astype(jnp.float32)], axis=0
    )
    conv = taps[0] * extended[:-2] + taps[1] * extended[1:-1] + taps[2] * extended[2:]
    gated = (c_part * conv).astype(jnp.bfloat16)
    resid = source + jnp.dot(gated, full[3], preferred_element_type=jnp.float32)
    scale_two, normed_two_f = norm_rows(resid, gain_two)
    normed_two = normed_two_f.astype(jnp.bfloat16)
    gate = jnp.dot(normed_two, full[5], preferred_element_type=jnp.float32)
    upper = jnp.dot(normed_two, full[6], preferred_element_type=jnp.float32)
    sigma = jax.nn.sigmoid(gate)
    swish = gate * sigma
    act = (swish * upper).astype(jnp.bfloat16)
    ffo = jnp.dot(act, full[7], preferred_element_type=jnp.float32)
    mixed = (keep * (resid + ffo)).astype(jnp.bfloat16)
    back_full = (
        lax.all_gather(norm1_gain, "shard", axis=0, tiled=True),
        lax.all_gather(in_proj, "shard", axis=0, tiled=True),
        lax.all_gather(conv_weight, "shard", axis=1, tiled=True),
        lax.all_gather(out_proj, "shard", axis=0, tiled=True),
        lax.all_gather(norm2_gain, "shard", axis=0, tiled=True),
        lax.all_gather(w_gate, "shard", axis=0, tiled=True),
        lax.all_gather(w_up, "shard", axis=0, tiled=True),
        lax.all_gather(w_down, "shard", axis=0, tiled=True),
    )
    grad_out = keep * cotangent.astype(jnp.float32)
    d_ffo = grad_out.astype(jnp.bfloat16)
    d_down = weight_grad(act, d_ffo)
    d_act = input_grad(d_ffo, back_full[7])
    d_gate = (d_act * upper * sigma * (1.0 + gate * (1.0 - sigma))).astype(jnp.bfloat16)
    d_up = (d_act * swish).astype(jnp.bfloat16)
    d_gate_w = weight_grad(normed_two, d_gate)
    d_up_w = weight_grad(normed_two, d_up)
    d_normed_two = input_grad(d_gate, back_full[5]) + input_grad(d_up, back_full[6])
    d_resid_norm, d_gain_two = norm_back(
        resid, scale_two, back_full[4].astype(jnp.float32), d_normed_two
    )
    d_resid = grad_out + d_resid_norm
    d_mix = d_resid.astype(jnp.bfloat16)
    d_proj_out = weight_grad(gated, d_mix)
    d_gated = input_grad(d_mix, back_full[3])
    back_taps = back_full[2].astype(jnp.float32)
    d_c = d_gated * conv
    d_conv = d_gated * c_part
    d_taps = jnp.stack(
        [
            jnp.sum(d_conv * extended[:-2], axis=0),
            jnp.sum(d_conv * extended[1:-1], axis=0),
            jnp.sum(d_conv * extended[2:], axis=0),
        ],
        axis=0,
    )
    zero_pair = jnp.zeros((2, width), jnp.float32)
    d_extended = jnp.concatenate([back_taps[0] * d_conv, zero_pair], axis=0)
    d_extended = d_extended + jnp.concatenate(
        [zero_pair[:1], back_taps[1] * d_conv, zero_pair[:1]], axis=0
    )
    d_extended = d_extended + jnp.concatenate([zero_pair, back_taps[2] * d_conv], axis=0)
    returned = from_behind(d_extended[:2] * inside, "shard", -1)
    d_product = d_extended[2:] + jnp.concatenate(
        [jnp.zeros((rows - 2, width), jnp.float32), returned], axis=0
    )
    d_bcx = jnp.concatenate([d_product * x_part, d_c, d_product * b_part], axis=1).astype(
        jnp.bfloat16
    )
    d_proj_in = weight_grad(normed, d_bcx)
    d_normed = input_grad(d_bcx, back_full[1])
    d_source, d_gain_one = norm_back(source, scale_one, back_full[0].astype(jnp.float32), d_normed)
    d_tokens = d_resid + d_source
    shares = (
        lax.psum_scatter(d_gain_one, "shard", scatter_dimension=0, tiled=True),
        lax.psum_scatter(d_proj_in, "shard", scatter_dimension=0, tiled=True),
        lax.psum_scatter(d_taps, "shard", scatter_dimension=1, tiled=True),
        lax.psum_scatter(d_proj_out, "shard", scatter_dimension=0, tiled=True),
        lax.psum_scatter(d_gain_two, "shard", scatter_dimension=0, tiled=True),
        lax.psum_scatter(d_gate_w, "shard", scatter_dimension=0, tiled=True),
        lax.psum_scatter(d_up_w, "shard", scatter_dimension=0, tiled=True),
        lax.psum_scatter(d_down, "shard", scatter_dimension=0, tiled=True),
    )
    summed = (
        lax.psum(shares[0].astype(jnp.bfloat16), "rep").astype(jnp.float32),
        lax.psum(shares[1].astype(jnp.bfloat16), "rep").astype(jnp.float32),
        lax.psum(shares[2].astype(jnp.bfloat16), "rep").astype(jnp.float32),
        lax.psum(shares[3].astype(jnp.bfloat16), "rep").astype(jnp.float32),
        lax.psum(shares[4].astype(jnp.bfloat16), "rep").astype(jnp.float32),
        lax.psum(shares[5].astype(jnp.bfloat16), "rep").astype(jnp.float32),
        lax.psum(shares[6].astype(jnp.bfloat16), "rep").astype(jnp.float32),
        lax.psum(shares[7].astype(jnp.bfloat16), "rep").astype(jnp.float32),
    )
    return (
        mixed,
        d_tokens,
        summed[0],
        summed[1],
        summed[2],
        summed[3],
        summed[4],
        summed[5],
        summed[6],
        summed[7],
    )


def solution(mesh):
    placed = (
        P(("rep", "shard"), None),
        P(),
        P("shard"),
        P("shard", None),
        P(None, "shard"),
        P("shard", None),
        P("shard"),
        P("shard", None),
        P("shard", None),
        P("shard", None),
        P(("rep", "shard"), None),
    )
    return jax.shard_map(
        body,
        mesh=mesh,
        in_specs=placed,
        out_specs=(
            P(("rep", "shard"), None),
            P(("rep", "shard"), None),
            P("shard"),
            P("shard", None),
            P(None, "shard"),
            P("shard", None),
            P("shard"),
            P("shard", None),
            P("shard", None),
            P("shard", None),
        ),
        check_vma=False,
    )
```

profile of v0, /device:TPU:1, one launch (start us, length us, event | category | flops | bytes accessed | tf_op | source)
XLA Modules:
  0.0 2018.3 jit_solution(17187808941637915131)
XLA Ops:
  14.3 165.4 %all-reduce.8 = (bf16[1024]{0:T(1024)(128)(2,1)S(1)}, bf16[1024]{0:T(1024)(128)(2,1)S(1)}) all-reduce(bf16[1024]{0:T(1024)(128)(2,1)S(1)} %dynamic-update-slice, bf16[1024]{0:T(1024)(128)(2,1)S(1)} %dynamic-update-slice.1), channel_id=1, replica_groups=mesh['rep'=2,'shard'=64] {'shard'}, use_global_device_ids=true, to_apply=%add.3 | all-reduce | flops 2048 | bytes 8192
  179.7 95.7 %all-gather = bf16[64,16,3]{1,2,0:T(4,128)(2,1)S(1)} all-gather(bf16[1,16,3]{1,2,0:T(4,128)(2,1)} %bitcast.50), channel_id=1, replica_groups=mesh['rep'=2,'shard'=64] {'shard'}, dimensions={0}, use_global_device_ids=true | all-gather | bytes 6240 | tf_op jit(solution)/shard_map/all_gather | solution.py:63
  279.1 4.8 fusion.26
  286.2 5.3 collective-permute-start
  298.6 9.0 fusion.34
  307.6 26.2 %all-gather.13.cloned.1.call-done = bf16[1024,4608]{1,0:T(8,128)(2,1)} async-done(((bf16[16,4608]{1,0:T(8,128)(2,1)}), bf16[1024,4608]{1,0:T(8,128)(2,1)}) %all-gather.13.cloned.1.call-update) | async-done | bytes 9437200 | tf_op jit(solution)/shard_map/all_gather | solution.py:67
  333.8 7.9 fusion.35
  341.7 78.0 %all-gather.15.cloned.1.call-done = bf16[4608,1024]{1,0:T(8,128)(2,1)} async-done(((bf16[72,1024]{1,0:T(8,128)(2,1)}), bf16[4608,1024]{1,0:T(8,128)(2,1)}) %all-gather.15.cloned.1.call-update) | async-done | bytes 9437200 | tf_op jit(solution)/shard_map/all_gather | solution.py:68
  419.7 13.3 multiply_convert_fusion
  433.0 6.9 fusion.36
  456.2 6.4 fusion.15
  462.7 9.8 fusion.37
  472.5 9.9 fusion.38
  483.5 9.9 fusion.21
  498.2 8.3 fusion.2
  506.4 5.1 fusion.13
  511.5 161.2 %all-reduce.7 = (bf16[1024]{0:T(1024)(128)(2,1)S(1)}, bf16[1024]{0:T(1024)(128)(2,1)S(1)}) all-reduce(f32[1024]{0:T(1024)S(1)} %get-tuple-element.14, f32[1024]{0:T(1024)S(1)} %get-tuple-element.12), channel_id=2, replica_groups=mesh['rep'=2,'shard'=64] {'shard'}, use_global_device_ids=true, to_apply=%region_6.7.clone | all-reduce | flops 2048 | bytes 12288
  674.5 188.1 %reduce-scatter.13.cloned.1.call-done = f32[16,4608]{1,0:T(8,128)} async-done(((f32[1024,4608]{1,0:T(8,128)}), f32[16,4608]{1,0:T(8,128)}) %reduce-scatter.13.cloned.1.call-update) | async-done | bytes 294928 | tf_op jit(solution)/shard_map/reduce_scatter | solution.py:157
  864.3 218.4 %reduce-scatter.15.cloned.1.call-done = f32[16,4608]{1,0:T(8,128)} async-done(((f32[1024,4608]{1,0:T(8,128)}), f32[16,4608]{1,0:T(8,128)}) %reduce-scatter.15.cloned.1.call-update) | async-done | bytes 294928 | tf_op jit(solution)/shard_map/reduce_scatter | solution.py:158
  1084.3 217.5 %reduce-scatter.17.cloned.1.call-done = f32[72,1024]{1,0:T(8,128)} async-done(((f32[4608,1024]{1,0:T(8,128)}), f32[72,1024]{1,0:T(8,128)}) %reduce-scatter.17.cloned.1.call-update) | async-done | bytes 294928 | tf_op jit(solution)/shard_map/reduce_scatter | solution.py:159
  1303.4 324.2 %reduce-scatter.19.cloned.1.call-done = f32[16,3]{1,0:T(8,128)} async-done(((f32[1024,3]{1,0:T(8,128)}), f32[16,3]{1,0:T(8,128)}) %reduce-scatter.19.cloned.1.call-update) | async-done | bytes 208
  1628.4 334.7 %reduce-scatter.11.cloned.1.call-done = f32[16,1024]{1,0:T(8,128)} async-done(((f32[1024,1024]{1,0:T(8,128)}), f32[16,1024]{1,0:T(8,128)}) %reduce-scatter.11.cloned.1.call-update) | async-done | bytes 65552 | tf_op jit(solution)/shard_map/reduce_scatter | solution.py:155
  1965.3 6.7 all-reduce.9
  1974.2 30.8 %all-reduce.13.cloned.1.call-done = (bf16[16,3072]{1,0:T(8,128)(2,1)}, bf16[16,4608]{1,0:T(8,128)(2,1)}, bf16[16,4608]{1,0:T(8,128)(2,1)}, bf16[72,1024]{1,0:T(8,128)(2,1)}) async-done(((bf16[16,3072]{1,0:T(8,128)(2,1)}, bf16[16,4608]{1,0:T(8,128)(2,1)}, bf16[16,4608]{1,0:T(8,128)(2,1)}, bf16[72,1024]{1,0:T(8,128)(2,1)}), (bf16[16,3072]{1,0:T(8,128)(2,1)}, bf16[16,4608]{1,0:T(8,128)(2,1)}, ...) | async-done | bytes 540688 | tf_op jit(solution)/shard_map/psum | solution.py:163
  (124 shorter events, 58.3 us)
Async XLA Ops:
  7.2 271.9 %all-gather.7.cloned.1.call-start = ((), (), s32[]{:S(2)}) async-start(), calls=%async_computation.6 | async-start | bytes 6389760 | tf_op jit(solution)/shard_map/all_gather | solution.py:62
  7.9 287.9 %all-gather.9.cloned.1.call-start = ((), (), s32[]{:S(2)}) async-start(), calls=%async_computation.7 | async-start | bytes 2129920 | tf_op jit(solution)/shard_map/all_gather | solution.py:64
  8.7 290.0 %all-gather.11.cloned.1.call-start = ((), (), s32[]{:S(2)}) async-start(), calls=%async_computation.8 | async-start | bytes 9584640 | tf_op jit(solution)/shard_map/all_gather | solution.py:66
  9.4 324.4 %all-gather.13.cloned.1.call-start = ((), (), s32[]{:S(2)}) async-start(), calls=%async_computation.9 | async-start | bytes 9584640 | tf_op jit(solution)/shard_map/all_gather | solution.py:67
  10.0 409.7 %all-gather.15.cloned.1.call-start = ((), (), s32[]{:S(2)}) async-start(), calls=%async_computation.10 | async-start | bytes 9584640 | tf_op jit(solution)/shard_map/all_gather | solution.py:68
  10.6 662.3 %reduce-scatter.9.cloned.1.call-start = ((), (), s32[]{:S(2)}) async-start(), calls=%async_computation.11 | async-start | bytes 12779520 | tf_op jit(solution)/shard_map/reduce_scatter | solution.py:153
  283.9 11.8 copy-start
  286.2 5.8 collective-permute-start
  307.6 112.1 %copy-start.12 = (bf16[256,1024]{1,0:T(8,128)(2,1)S(1)}, bf16[256,1024]{1,0:T(8,128)(2,1)}, u32[]{:S(2)}) copy-start(bf16[256,1024]{1,0:T(8,128)(2,1)} %param.21) | copy-start | bytes 1572868
  433.0 7.0 copy-start.9
  433.0 7.0 copy-start.8
  433.0 8.1 copy-start.2
  447.9 7.3 copy-start.14
  448.4 6.5 collective-permute-start.1
  451.2 5.0 copy-start.5
  462.6 400.0 %reduce-scatter.13.cloned.1.call-start = ((), (), s32[]{:S(2)}) async-start(), calls=%async_computation.13 | async-start | bytes 19169280 | tf_op jit(solution)/shard_map/reduce_scatter | solution.py:157
  472.5 610.2 %reduce-scatter.15.cloned.1.call-start = ((), (), s32[]{:S(2)}) async-start(), calls=%async_computation.14 | async-start | bytes 19169280 | tf_op jit(solution)/shard_map/reduce_scatter | solution.py:158
  482.5 819.3 %reduce-scatter.17.cloned.1.call-start = ((), (), s32[]{:S(2)}) async-start(), calls=%async_computation.15 | async-start | bytes 19169280 | tf_op jit(solution)/shard_map/reduce_scatter | solution.py:159
  493.4 1134.2 %reduce-scatter.19.cloned.1.call-start = ((), (), s32[]{:S(2)}) async-start(), calls=%async_computation.16 | async-start | bytes 532480
  494.6 1468.6 %reduce-scatter.11.cloned.1.call-start = ((), (), s32[]{:S(2)}) async-start(), calls=%async_computation.12 | async-start | bytes 4259840 | tf_op jit(solution)/shard_map/reduce_scatter | solution.py:155
  497.4 1507.5 %all-reduce.13.cloned.1.call-start = ((), (), s32[]{:S(2)}) async-start(), calls=%async_computation.17 | async-start | bytes 1081344 | tf_op jit(solution)/shard_map/psum | solution.py:163
  498.1 8.3 copy-start.15
  498.1 8.3 copy-start.17
  498.1 8.3 copy-start.19
  (10 other events, 18.1 us)
Sparse Core Ops, SparseCore 0:
  11.1 82.2 all-gather.6
  96.4 65.0 all-gather.8
  164.6 83.2 all-gather.10
  250.8 82.9 all-gather.12
  336.7 82.9 all-gather.14
  462.7 180.8 reduce-scatter.8
  649.7 212.8 reduce-scatter.12
  869.7 212.8 reduce-scatter.14
  1088.7 213.0 reduce-scatter.16
  1304.1 323.5 reduce-scatter.18
  1630.0 333.0 reduce-scatter.10
  1967.0 37.8 all-reduce.12
where the time goes:
time: 2020 us
  waiting for transfers between devices  1430 us (71%)
  blocking collectives  429 us (21%)
  matrix products  100 us (5%)
  other arithmetic  27.5 us (1%)
    reduce_scatter x1, waiting for transfers between devices, body(): lax.psum_scatter(d_proj_out, 'shard', scatter_dimension=0, tiled=True)  335 us
    unnamed x13, waiting for transfers between devices  327 us
    unnamed x2, blocking collectives  327 us
    reduce_scatter x1, waiting for transfers between devices, body(): lax.psum_scatter(d_up_w, 'shard', scatter_dimension=0, tiled=True)  218 us
    reduce_scatter x1, waiting for transfers between devices, body(): lax.psum_scatter(d_down, 'shard', scatter_dimension=0, tiled=True)  217 us
    reduce_scatter x1, waiting for transfers between devices, body(): lax.psum_scatter(d_gate_w, 'shard', scatter_dimension=0, tiled=True)  188 us
    all_gather x1, blocking collectives, body(): lax.all_gather(conv_weight, 'shard', axis=1, tiled=True)  95.7 us
    all_gather x1, waiting for transfers between devices, body(): lax.all_gather(w_down, 'shard', axis=0, tiled=True)  78 us
  transfers between devices with their start and end apart: 14, of which 10 were waited for; matrix products, arithmetic and copies ran while one was open for 5% of the time, Pallas kernels for 0%

commit v1 on v0

v1 whole, which is shorter than its diff:
```python
import functools
import jax, jax.numpy as jnp
from jax import lax
from jax.experimental import pallas as pl
from jax.experimental.pallas import tpu as pltpu
from jax.sharding import PartitionSpec as P
MESH = pl.DeviceIdType.MESH
C1 = 2176; HALF = 1152; CAT = 6784; UNIT = 32; DUNIT = 144
COPIES = 160

def spot():
    rep = lax.axis_index("rep"); s = lax.axis_index("shard")
    return (s // 4) % 4, s // 16, ((s // 2) % 2) * 2 + rep, s % 2

def device(x, y, z, c):
    return (z % 2, ((y * 4 + x) * 2 + z // 2) * 2 + c)

def moved(x, y, z, c, axis, step):
    if axis == "x": return device((x + step + 4) % 4, y, z, c)
    return device(x, (y + step + 4) % 4, z, c)

def greet(devices):
    bar = pltpu.get_barrier_semaphore()
    for d in devices:
        pl.semaphore_signal(bar, inc=1, device_id=d, device_id_type=MESH)
    pl.semaphore_wait(bar, len(devices))

class Wire:
    def __init__(self, ss, rs): self.ss, self.rs, self.sent = ss, rs, []
    def send(self, src, dst, dev):
        i = len(self.sent)
        cp = pltpu.make_async_remote_copy(src_ref=src, dst_ref=dst, send_sem=self.ss.at[i], recv_sem=self.rs.at[i], device_id=dev, device_id_type=MESH)
        cp.start(); self.sent.append(cp); return cp
    def drain(self):
        for cp in self.sent: cp.wait_send()

def gather_kernel(cat_in, down_in, wcat, wd, wor, wdr, dnf, dnb, ss, rs, ls):
    x, y, z, c = spot()
    hi = z // 2
    s = ((y * 4 + x) * 2 + hi) * 2 + c
    k = s // 2
    pair = device(x, y, z + 1 - 2 * (z % 2), c)
    cross = device(x, y, 3 - z, c)
    other = device(x, y, z, 1 - c)
    go = {(a, st): moved(x, y, z, c, a, st) for a in "xy" for st in (1, -1)}
    greet(list(go.values()) + [pair, cross, other])
    w = Wire(ss, rs)
    rows = pl.ds(pl.multiple_of(16 * s, 16), 16)
    lc = pltpu.make_async_copy(cat_in.at[c], wcat.at[rows, :], ls.at[0]); lc.start()
    r0 = w.send(cat_in.at[1 - c], wcat.at[rows, :], other)
    dr = pl.ds(pl.multiple_of(72 * c, 8), 72)
    ld = pltpu.make_async_copy(down_in.at[c], dnf.at[dr, :], ls.at[1]); ld.start()
    r1 = w.send(down_in.at[1 - c], dnf.at[dr, :], other)
    lc.wait(); r0.wait_recv()
    urow = pl.ds(pl.multiple_of(UNIT * k, UNIT), UNIT)
    drow = pl.ds(pl.multiple_of(DUNIT * k, 16), DUNIT)
    z1 = w.send(wcat.at[urow, pl.ds(0, C1)], wcat.at[urow, pl.ds(0, C1)], cross)
    z2 = w.send(wcat.at[urow, pl.ds(C1, CAT - C1)], wcat.at[urow, pl.ds(C1, CAT - C1)], cross)
    ld.wait(); r1.wait_recv()
    dnb[...] = dnf[...].astype(jnp.bfloat16)
    ldb = pltpu.make_async_copy(dnb, wd.at[drow, :], ls.at[2]); ldb.start()
    z3 = w.send(dnb, wd.at[drow, :], cross)
    flows = [
        dict(buf=wcat, unit=UNIT, col=0, width=C1, order="xy", need=[z1], fwd=None),
        dict(buf=wcat, unit=UNIT, col=C1 + HALF * (z % 2), width=HALF, order="yx", need=[z2], fwd=pair),
        dict(buf=wcat, unit=UNIT, col=C1 + 2 * HALF + HALF * hi, width=HALF, order="xy", need=[], fwd=cross),
        dict(buf=wd, unit=DUNIT, col=0, width=512, order="yx", need=[z3], fwd=None),
    ]
    def block(f, da, db, unit=None):
        a, b = f["order"]
        pos = {"x": x, "y": y}
        pos[a] = (pos[a] + da + 4) % 4
        pos[b] = (pos[b] + db + 4) % 4
        u = f["unit"]
        row = (pos["y"] * 4 + pos["x"]) * (2 * u)
        n = 2 * u
        if unit is not None: row, n = row + unit * u, u
        col = f["col"] if isinstance(f["col"], int) else pl.multiple_of(f["col"], 128)
        return f["buf"].at[pl.ds(pl.multiple_of(row, 16), n), pl.ds(col, f["width"])]
    def push(f, da, db, dev, unit=None):
        v = block(f, da, db, unit)
        return w.send(v, v, dev)
    def fwd(f, da, db):
        if f["fwd"] is not None: f.setdefault("z", []).append(push(f, da, db, f["fwd"]))
    def open2(f, j):
        b = f["order"][1]
        f[("p", j)] = push(f, j, 0, go[(b, 1)])
        f[("m", j)] = push(f, j, 0, go[(b, -1)])
    for n, f in enumerate(flows):
        for q in f["need"]: q.wait_recv()
        if n == 3: ldb.wait()
        a = f["order"][0]
        f["p"] = push(f, 0, 0, go[(a, 1)])
        f["m"] = push(f, 0, 0, go[(a, -1)])
        open2(f, 0)
    for f in flows:
        a = f["order"][0]
        f["p"].wait_recv(); f["p2"] = push(f, -1, 0, go[(a, 1)], 0)
        f["m"].wait_recv(); f["m2"] = push(f, 1, 0, go[(a, -1)], 1)
        open2(f, -1); open2(f, 1)
        fwd(f, -1, 0); fwd(f, 1, 0)
    for f in flows:
        f["p2"].wait_recv(); f["m2"].wait_recv()
        open2(f, 2); fwd(f, 2, 0)
    for j in (0, -1, 1, 2):
        for f in flows:
            b = f["order"][1]
            f[("p", j)].wait_recv(); f[("p2", j)] = push(f, j, -1, go[(b, 1)], 0)
            f[("m", j)].wait_recv(); f[("m2", j)] = push(f, j, 1, go[(b, -1)], 1)
            fwd(f, j, -1); fwd(f, j, 1)
    for j in (0, -1, 1, 2):
        for f in flows:
            f[("p2", j)].wait_recv(); f[("m2", j)].wait_recv()
            fwd(f, j, 2)
    for f in flows:
        for q in f.get("z", []): q.wait_recv()
    a = w.send(wcat.at[pl.ds(pl.multiple_of(512 * (1 - c), 512), 512), pl.ds(1536, 512)], wor, other)
    b = w.send(wd.at[pl.ds(pl.multiple_of(2304 * (1 - c), 2304), 2304), :], wdr, other)
    a.wait_recv(); b.wait_recv()
    w.drain()

def gather_all(cat, down):
    return pl.pallas_call(
        gather_kernel,
        out_shape=(jax.ShapeDtypeStruct((1024, CAT), jnp.bfloat16), jax.ShapeDtypeStruct((4608, 512), jnp.bfloat16),
            jax.ShapeDtypeStruct((512, 512), jnp.bfloat16), jax.ShapeDtypeStruct((2304, 512), jnp.bfloat16)),
        in_specs=[pl.BlockSpec(memory_space=pl.ANY)] * 2,
        out_specs=(pl.BlockSpec(memory_space=pl.ANY),) * 4,
        scratch_shapes=[pltpu.VMEM((144, 512), jnp.float32), pltpu.VMEM((144, 512), jnp.bfloat16),
            pltpu.SemaphoreType.DMA((COPIES,)), pltpu.SemaphoreType.DMA((COPIES,)), pltpu.SemaphoreType.DMA((3,))],
        compiler_params=pltpu.CompilerParams(collective_id=1, has_side_effects=True, vmem_limit_bytes=32 * 2**20),
        name="gather")(cat, down)

def prepare(norm1_gain, in_proj, conv_weight, out_proj, norm2_gain, w_gate, w_up, w_down):
    small = jnp.stack([norm1_gain, norm2_gain, conv_weight[0], conv_weight[1], conv_weight[2]], axis=1)
    small = jnp.pad(small, ((0, 0), (0, 123)))
    cat = jnp.stack([jnp.concatenate([in_proj[:, 512*p:512*p+512], in_proj[:, 1024+512*p:1536+512*p], in_proj[:, 2048+512*p:2560+512*p],
        out_proj[:, 512*p:512*p+512], small, w_gate[:, 2304*p:2304*p+2304], w_up[:, 2304*p:2304*p+2304]], axis=1) for p in (0, 1)])
    down = jnp.stack([w_down[:, :512], w_down[:, 512:]]).astype(jnp.float32)
    return cat, down

JS = (2, -1, 1, 0)

def add_into(dst, srcs, rows, step=16):
    def body(i, _):
        r = pl.ds(pl.multiple_of(i * step, step), step)
        t = dst[r, :].astype(jnp.float32)
        for q in srcs: t = t + q[r, :].astype(jnp.float32)
        dst[r, :] = t.astype(jnp.bfloat16)
        return 0
    lax.fori_loop(0, rows // step, body, 0)

def scatter_kernel(gin, gout, gsm, gg, gu, gd, ocat, odn,
                   G1, GG, GU, GD, L1, LG, LU, LD, M1, MG, MU, MD,
                   d1, dg, du, dd, fcat, fdn, ss, rs, ls):
    x, y, z, c = spot()
    hi = z // 2
    pair = device(x, y, z + 1 - 2 * (z % 2), c)
    cross = device(x, y, 3 - z, c)
    other = device(x, y, z, 1 - c)
    go = {(a, st): moved(x, y, z, c, a, st) for a in "xy" for st in (1, -1)}
    greet(list(go.values()) + [pair, cross, other])
    w = Wire(ss, rs)
    nl = [0]
    def local(src, dst):
        cp = pltpu.make_async_copy(src, dst, ls.at[nl[0]]); nl[0] += 1; cp.start(); return cp
    rd = w.send(gd.at[1 - c], GD.at[pl.ds(2 * c, 2)], other)
    ld = local(gd.at[c], GD.at[pl.ds(2 * c, 2)])
    lg = [local(gg.at[:, :, :, pl.ds(h * HALF, HALF)], GG.at[h]) for h in (0, 1)]
    lu = [local(gu.at[:, :, :, pl.ds(h * HALF, HALF)], GU.at[h]) for h in (0, 1)]
    ro = w.send(gout.at[1 - c], G1.at[pl.ds(2 * c, 2), :, :, pl.ds(1536, 512)], other)
    lo = local(gout.at[c], G1.at[pl.ds(2 * c, 2), :, :, pl.ds(1536, 512)])
    li = local(gin, G1.at[:, :, :, pl.ds(0, 1536)])
    lsm = local(gsm, G1.at[:, :, :, pl.ds(2048, 128)])
    zl = z % 2
    fd = dict(G=GD, L=LD, M=MD, unit=DUNIT, order="yx")
    fg = dict(G=GG.at[zl], L=LG.at[zl], M=MG, unit=UNIT, order="yx")
    fu = dict(G=GU.at[hi], L=LU.at[hi], M=MU, unit=UNIT, order="xy")
    f1 = dict(G=G1, L=L1, M=M1, unit=UNIT, order="xy")
    flows = [fd, fg, fu, f1]
    def at(f, da, db):
        a, b = f["order"]
        pos = {"x": x, "y": y}
        pos[a] = (pos[a] + da + 4) % 4
        pos[b] = (pos[b] + db + 4) % 4
        return pos["y"], pos["x"]
    def line(f, j):
        return (x + j + 4) % 4 if f["order"] == "xy" else (y + j + 4) % 4
    for q in lg: q.wait()
    for q in lu: q.wait()
    for j in JS:
        yj = line(fg, j); fg[("A", j)] = w.send(GG.at[1 - zl, yj], LG.at[zl, yj], pair)
        xj = line(fu, j); fu[("A", j)] = w.send(GU.at[1 - hi, :, xj], LU.at[hi, :, xj], cross)
    def absorb(f, j):
        if ("A", j) not in f: return
        f[("A", j)].wait_recv()
        l = line(f, j)
        for i in range(4):
            if f is fg: add_into(GG.at[zl, l, i], [LG.at[1 - zl, l, i]], 64)
            else: add_into(GU.at[hi, i, l], [LU.at[1 - hi, i, l]], 64)
    def part(ref, f, pos, u):
        return ref.at[pos[0], pos[1], pl.ds(u * f["unit"], f["unit"])]
    ready = {id(fd): [ld.wait, rd.wait_recv], id(f1): [lo.wait, li.wait, lsm.wait, ro.wait_recv]}
    for f in flows:
        for q in ready.get(id(f), []): q()
        ready[id(f)] = []
        b = f["order"][1]
        for j in JS:
            absorb(f, j)
            p = at(f, j, 2)
            f[("s", j)] = w.send(part(f["G"], f, p, 0), part(f["L"], f, p, 0), go[(b, 1)])
            f[("t", j)] = w.send(part(f["G"], f, p, 1), part(f["L"], f, p, 1), go[(b, -1)])
    for j in JS:
        for f in flows:
            b = f["order"][1]
            f[("s", j)].wait_recv(); p = at(f, j, 1)
            add_into(part(f["G"], f, p, 0), [part(f["L"], f, p, 0)], f["unit"])
            f[("s2", j)] = w.send(f["G"].at[p[0], p[1]], f["L"].at[p[0], p[1]], go[(b, 1)])
            f[("t", j)].wait_recv(); p = at(f, j, -1)
            add_into(part(f["G"], f, p, 1), [part(f["L"], f, p, 1)], f["unit"])
            o = at(f, j, 1)
            f[("t2", j)] = w.send(f["G"].at[p[0], p[1]], f["L"].at[o[0], o[1]], go[(b, -1)])
    for j in JS:
        for f in flows:
            a = f["order"][0]
            f[("s2", j)].wait_recv(); f[("t2", j)].wait_recv()
            p = at(f, j, 0); o = at(f, j, 2)
            add_into(f["G"].at[p[0], p[1]], [f["L"].at[p[0], p[1]], f["L"].at[o[0], o[1]]], 2 * f["unit"])
            u = f["unit"]; M = f["M"]
            if j == 2:
                f["c"] = w.send(part(f["G"], f, p, 0), M.at[pl.ds(0, u)], go[(a, 1)])
                f["d"] = w.send(part(f["G"], f, p, 1), M.at[pl.ds(u, u)], go[(a, -1)])
            elif j == 1:
                f["c"].wait_recv(); add_into(part(f["G"], f, p, 0), [M.at[pl.ds(0, u)]], u)
                f["c2"] = w.send(f["G"].at[p[0], p[1]], M.at[pl.ds(2 * u, 2 * u)], go[(a, 1)])
            elif j == -1:
                f["d"].wait_recv(); add_into(part(f["G"], f, p, 1), [M.at[pl.ds(u, u)]], u)
                f["d2"] = w.send(f["G"].at[p[0], p[1]], M.at[pl.ds(4 * u, 2 * u)], go[(a, -1)])
    for f in flows:
        f["c2"].wait_recv(); f["d2"].wait_recv()
        u = f["unit"]; M = f["M"]; mine = f["G"].at[y, x]
        add_into(mine, [M.at[pl.ds(2 * u, 2 * u)], M.at[pl.ds(4 * u, 2 * u)]], 2 * u)
        away = mine.at[pl.ds(u * (1 - hi), u)]
        if f is fd: f["e"] = w.send(away, dd.at[0], cross)
        if f is f1: f["e"] = w.send(away, d1.at[0], cross)
        if f is fu: f["e"] = w.send(away, du.at[0, hi], cross)
        if f is fg: f["e"] = w.send(mine, dg.at[0, zl], pair)
    own = lambda f: f["G"].at[y, x, pl.ds(f["unit"] * hi, f["unit"])]
    fd["e"].wait_recv(); add_into(own(fd), [dd.at[0]], DUNIT)
    fd["e2"] = w.send(own(fd), dd.at[1], pair)
    fg["e"].wait_recv()
    fg["e2"] = w.send(fg["G"].at[y, x, pl.ds(UNIT * (1 - hi), UNIT)], dg.at[1, zl, pl.ds(0, UNIT)], cross)
    fg["e3"] = w.send(dg.at[0, 1 - zl, pl.ds(UNIT * (1 - hi), UNIT)], dg.at[1, 1 - zl, pl.ds(0, UNIT)], cross)
    fu["e"].wait_recv()
    fu["e2"] = w.send(own(fu), du.at[1, hi], pair)
    fu["e3"] = w.send(du.at[0, 1 - hi], du.at[1, 1 - hi], pair)
    f1["e"].wait_recv(); add_into(own(f1), [d1.at[0]], UNIT)
    f1["e2"] = w.send(own(f1), d1.at[1], pair)
    f32 = lambda v: v.astype(jnp.float32)
    fd["e2"].wait_recv()
    fdn[...] = f32(own(fd)[...]) + f32(dd[1])
    o1 = w.send(fdn.at[pl.ds(pl.multiple_of(72 * (1 - c), 8), 72)], odn.at[c], other)
    q1 = local(fdn.at[pl.ds(pl.multiple_of(72 * c, 8), 72)], odn.at[c])
    for q in ("e2", "e3"): fg[q].wait_recv(); fu[q].wait_recv()
    cg = C1 + HALF * zl; cgo = C1 + HALF * (1 - zl)
    cu = C1 + 2 * HALF + HALF * hi; cuo = C1 + 2 * HALF + HALF * (1 - hi)
    m128 = lambda v: pl.ds(pl.multiple_of(v, 128), HALF)
    fcat[:, m128(cg)] = f32(own(fg)[...]) + f32(dg[1, zl, pl.ds(0, UNIT), :])
    fcat[:, m128(cgo)] = f32(dg[0, 1 - zl, pl.ds(UNIT * hi, UNIT), :]) + f32(dg[1, 1 - zl, pl.ds(0, UNIT), :])
    fcat[:, m128(cu)] = f32(own(fu)[...]) + f32(du[1, hi])
    fcat[:, m128(cuo)] = f32(du[0, 1 - hi]) + f32(du[1, 1 - hi])
    f1["e2"].wait_recv()
    fcat[:, pl.ds(0, C1)] = f32(own(f1)[...]) + f32(d1[1])
    o2 = w.send(fcat.at[pl.ds(pl.multiple_of(16 * (1 - c), 16), 16)], ocat.at[c], other)
    q2 = local(fcat.at[pl.ds(pl.multiple_of(16 * c, 16), 16)], ocat.at[c])
    q1.wait(); q2.wait(); o1.wait_recv(); o2.wait_recv()
    w.drain()

def scatter_all(gin, gout, gsm, gg, gu, gd):
    bf = jnp.bfloat16
    V = lambda *s: pltpu.VMEM(s, bf)
    grid = lambda v: v.reshape(4, 4, -1, v.shape[-1])
    half = lambda v: v.reshape(2, 2, 4, -1, 512)
    return pl.pallas_call(
        scatter_kernel,
        out_shape=(jax.ShapeDtypeStruct((2, 16, CAT), jnp.float32), jax.ShapeDtypeStruct((2, 72, 512), jnp.float32)),
        in_specs=[pl.BlockSpec(memory_space=pl.ANY)] * 6,
        out_specs=(pl.BlockSpec(memory_space=pl.ANY),) * 2,
        scratch_shapes=[V(4, 4, 64, C1), V(2, 4, 4, 64, HALF), V(2, 4, 4, 64, HALF), V(4, 4, 288, 512),
            V(4, 4, 64, C1), V(2, 4, 4, 64, HALF), V(2, 4, 4, 64, HALF), V(4, 4, 288, 512),
            V(192, C1), V(192, HALF), V(192, HALF), V(864, 512),
            V(2, UNIT, C1), V(2, 2, 64, HALF), V(2, 2, UNIT, HALF), V(2, DUNIT, 512),
            pltpu.VMEM((UNIT, CAT), jnp.float32), pltpu.VMEM((DUNIT, 512), jnp.float32),
            pltpu.SemaphoreType.DMA((COPIES,)), pltpu.SemaphoreType.DMA((COPIES,)), pltpu.SemaphoreType.DMA((12,))],
        compiler_params=pltpu.CompilerParams(collective_id=2, has_side_effects=True, vmem_limit_bytes=60 * 2**20),
        name="scatter")(grid(gin), half(gout), grid(gsm), grid(gg), grid(gu), half(gd))

def finish(ocat, odn):
    a, b = ocat[0], ocat[1]
    j = lambda o, n: [a[:, o:o + n], b[:, o:o + n]]
    d_in = jnp.concatenate(j(0, 512) + j(512, 512) + j(1024, 512), axis=1)
    d_out = jnp.concatenate(j(1536, 512), axis=1)
    sm = a[:, 2048:2053] + b[:, 2048:2053]
    d_gate = jnp.concatenate(j(C1, 2304), axis=1)
    d_up = jnp.concatenate(j(C1 + 2304, 2304), axis=1)
    d_down = jnp.concatenate([odn[0], odn[1]], axis=1)
    return sm[:, 0], d_in, sm[:, 2:5].T, d_out, sm[:, 1], d_gate, d_up, d_down

EPS = 1e-05

def swap(v):
    return lax.ppermute(v, "shard", [(s, s ^ 1) for s in range(64)])

def ordered(own, oth, c, axis=0):
    return jnp.where(c == 0, jnp.concatenate([own, oth], axis), jnp.concatenate([oth, own], axis))

def norm_rows(rows, gain):
    scale = lax.rsqrt(jnp.mean(rows * rows, axis=1, keepdims=True) + EPS)
    return scale, rows * scale * gain

def norm_back(rows, scale, gain, grad_norm):
    gain_grad = jnp.sum(grad_norm * rows * scale, axis=0)
    weighted = grad_norm * gain
    inner = jnp.mean(weighted * rows, axis=1, keepdims=True)
    return scale * weighted - rows * (scale * scale * scale) * inner, gain_grad

def dot(a, b): return jnp.dot(a, b, preferred_element_type=jnp.float32)
def tn(a, b): return lax.dot_general(a, b, (((0,), (0,)), ((), ())), preferred_element_type=jnp.float32)
def nt(a, b): return lax.dot_general(a, b, (((1,), (1,)), ((), ())), preferred_element_type=jnp.float32)

def share(part, c):
    n = part.shape[0] // 2
    own = lax.dynamic_slice_in_dim(part, n * c, n, 0)
    away = lax.dynamic_slice_in_dim(part, n * (1 - c), n, 0)
    return own + swap(away)

def middle(tokens, keep, cot, wcat, wd, wor, wdr):
    s_id = lax.axis_index("shard"); c = s_id % 2
    bf = jnp.bfloat16; f32 = jnp.float32
    inside = (s_id >= 2).astype(f32)
    small = wcat[:, 2048:2053].astype(f32).T
    g1, g2, taps = small[0], small[1], small[2:5]
    taps = lax.dynamic_slice_in_dim(taps, 512 * c, 512, 1)
    rows2 = lambda v, n: lax.dynamic_slice_in_dim(v, n * c, n, 0)
    w_in = wcat[:, :1536]
    w_out = ordered(rows2(wcat[:, 1536:2048], 512), wor, c, 1)
    w_dn = ordered(rows2(wd, 2304), wdr, c, 1)
    w_g, w_u = wcat[:, C1:C1 + 2304], wcat[:, C1 + 2304:]
    d_ffo_own = (keep * cot.astype(f32)).astype(bf)
    T = ordered(tokens, swap(tokens), c).astype(f32)
    d_ffo = ordered(d_ffo_own, swap(d_ffo_own), c)
    src = tokens.astype(f32)
    _, hf = norm_rows(T, g1); h = hf.astype(bf)
    s1, _ = norm_rows(src, g1)
    bcx = dot(h, w_in)
    B, C, X = bcx[:, :512], bcx[:, 512:1024], bcx[:, 1024:]
    bx = (B * X).astype(bf)
    edge = lax.ppermute(bx[510:], "shard", [(s, s + 2) for s in range(62)])
    ext = jnp.concatenate([edge.astype(f32) * inside, bx.astype(f32)], axis=0)
    conv = taps[0] * ext[:-2] + taps[1] * ext[1:-1] + taps[2] * ext[2:]
    y = (C * conv).astype(bf)
    resid = src + share(dot(y, w_out), c)
    s2, h2f = norm_rows(resid, g2)
    h2o = h2f.astype(bf)
    h2 = ordered(h2o, swap(h2o), c)
    gate = dot(h2, w_g); up = dot(h2, w_u)
    sg = jax.nn.sigmoid(gate); sw = gate * sg
    act = (sw * up).astype(bf)
    ffo = share(dot(act, w_dn), c)
    mixed = (keep * (resid + ffo)).astype(bf)
    d_down = tn(act, d_ffo).astype(bf)
    d_act = nt(d_ffo, w_dn)
    d_gate = (d_act * up * sg * (1.0 + gate * (1.0 - sg))).astype(bf)
    d_up = (d_act * sw).astype(bf)
    d_wg = tn(h2, d_gate).astype(bf); d_wu = tn(h2, d_up).astype(bf)
    d_h2 = share(nt(d_gate, w_g) + nt(d_up, w_u), c)
    d_rn, d_g2 = norm_back(resid, s2, g2, d_h2)
    d_resid = keep * cot.astype(f32) + d_rn
    dmo = d_resid.astype(bf)
    d_mix = ordered(dmo, swap(dmo), c)
    d_out = tn(y, d_mix).astype(bf)
    d_y = nt(d_mix, w_out)
    d_c = d_y * conv; d_conv = d_y * C
    d_taps = jnp.stack([jnp.sum(d_conv * ext[i:i + 512], axis=0) for i in range(3)])
    z2 = jnp.zeros((2, 512), f32)
    de = jnp.concatenate([taps[0] * d_conv, z2], 0) + jnp.concatenate([z2[:1], taps[1] * d_conv, z2[:1]], 0) + jnp.concatenate([z2, taps[2] * d_conv], 0)
    back = lax.ppermute(de[:2] * inside, "shard", [(s, s - 2) for s in range(2, 64)])
    d_bx = de[2:] + jnp.concatenate([jnp.zeros((510, 512), f32), back], 0)
    d_bcx = jnp.concatenate([d_bx * X, d_c, d_bx * B], axis=1).astype(bf)
    d_in = tn(h, d_bcx).astype(bf)
    d_h = share(nt(d_bcx, w_in), c)
    d_src, d_g1 = norm_back(src, s1, g1, d_h)
    d_tokens = d_resid + d_src
    dt = lax.dynamic_update_slice(jnp.zeros((3, 1024), f32), d_taps, (0, 512 * c))
    sm = jnp.concatenate([d_g1[None], d_g2[None], dt], 0).T.astype(bf)
    sm = jnp.pad(sm, ((0, 0), (0, 123)))
    cols = lambda v: jnp.stack([v[:, :512], v[:, 512:]])
    return mixed, d_tokens, d_in, cols(d_out), sm, d_wg, d_wu, cols(d_down)


def body(tokens, lengths, norm1_gain, in_proj, conv_weight, out_proj, norm2_gain, w_gate, w_up, w_down, cotangent):
    rows = tokens.shape[0]
    place = lax.axis_index("shard")
    slot = lax.axis_index("rep")
    slot_ids = jnp.arange(lengths.shape[0], dtype=jnp.int32)
    length = jnp.sum(jnp.where(slot_ids == slot, lengths, 0))
    valid = jnp.clip(length - place * rows, 0, rows)
    keep = (jnp.arange(rows, dtype=jnp.int32) < valid).astype(jnp.float32)[:, None]
    cat, down = prepare(norm1_gain, in_proj, conv_weight, out_proj, norm2_gain, w_gate, w_up, w_down)
    weights = gather_all(cat, down)
    mixed, d_tokens, *grads = middle(tokens, keep, cotangent, *weights)
    return (mixed, d_tokens) + finish(*scatter_all(*grads))

def solution(mesh):
    tok = P(("rep", "shard"), None)
    par = (P("shard"), P("shard", None), P(None, "shard"), P("shard", None), P("shard"), P("shard", None), P("shard", None), P("shard", None))
    return jax.shard_map(body, mesh=mesh, in_specs=(tok, P()) + par + (tok,), out_specs=(tok, tok) + par, check_vma=False)
```

time: 2020 us -> 408 us (0.20)
  waiting for transfers between devices: 1430 us -> 4.96 us
  blocking collectives: 429 us -> 0 us
  Pallas kernels: 0 us -> 259 us
  matrix products: 100 us -> 61 us
  local copies, waits for them, and re-layouts: 11.4 us -> 39.9 us
    reduce_scatter x5 -> x0, waiting for transfers between devices: 959 us -> none  [the longest x1 335 us: body(): lax.psum_scatter(d_proj_out, 'shard', scatter_dimension=0, tiled=True)]
    unnamed x13 -> x0, waiting for transfers between devices: 327 us -> none
    unnamed x2 -> x0, blocking collectives: 327 us -> none
    pallas_call x0 -> x2, Pallas kernels: none -> 259 us  [the longest x1 155 us: scatter_all(): pl.pallas_call(scatter_kernel, out_shape=(jax.ShapeDtypeStruct((2, 16, CA...]
    all_gather x5 -> x0, waiting for transfers between devices: 104 us -> none  [the longest x1 78 us: body(): lax.all_gather(w_down, 'shard', axis=0, tiled=True)]
    all_gather x1 -> x0, blocking collectives: 95.7 us -> none  [body(): lax.all_gather(conv_weight, 'shard', axis=1, tiled=True)]
    dot_general x15, matrix products: 100 us -> 61 us  [the longest x5 23.8 us: tn(): lax.dot_general(a, b, (((0,), (0,)), ((), ())), preferred_element_type=jn...]
    psum x1 -> x0, waiting for transfers between devices: 30.8 us -> none  [body(): lax.psum(shares[1].astype(jnp.bfloat16), 'rep').astype(jnp.float32)]
  transfers between devices with their start and end apart: 14 -> 10, of which waited for: 10 -> 2; matrix products, arithmetic and copies ran while one was open for 5% -> 15% of each run, Pallas kernels for 0% -> 26%
where the time goes in v1:
time: 408 us; the launch traced here: 401 us
  Pallas kernels  259 us (63%)
  matrix products  61 us (15%)
  local copies, waits for them, and re-layouts  39.9 us (10%)
  other arithmetic  24.1 us (6%)
  starting transfers between devices  9.86 us (2%)
  waiting for transfers between devices  4.96 us (1%)
    pallas_call x1, Pallas kernels, scatter_all(): pl.pallas_call(scatter_kernel, out_shape=(jax.ShapeDtypeStruct((2, 16, CA...  155 us
    pallas_call x1, Pallas kernels, gather_all(): pl.pallas_call(gather_kernel, out_shape=(jax.ShapeDtypeStruct((1024, CAT)...  104 us
    dot_general x5, matrix products, tn(): lax.dot_general(a, b, (((0,), (0,)), ((), ())), preferred_element_type=jn...  23.8 us
    dot_general x5, matrix products, dot(): return jnp.dot(a, b, preferred_element_type=jnp.float32)  21.1 us
    unnamed x76, local copies, waits for them, and re-layouts  20.6 us
    dot_general x5, matrix products, nt(): lax.dot_general(a, b, (((1,), (1,)), ((), ())), preferred_element_type=jn...  16.1 us
  transfers between devices with their start and end apart: 10, of which 2 were waited for; matrix products, arithmetic and copies ran while one was open for 15% of the time, Pallas kernels for 26%

profile of v1, /device:TPU:1, one launch (start us, length us, event | category | flops | bytes accessed | tf_op | source)
XLA Modules:
  0.0 401.1 jit_solution(3667291526762377695)
XLA Ops:
  12.1 104.3 %gather.1 = (bf16[1024,6784]{1,0:T(8,128)(2,1)S(1)}, bf16[4608,512]{1,0:T(8,128)(2,1)S(1)}, bf16[512,512]{1,0:T(8,128)(2,1)S(1)}, bf16[2304,512]{1,0:T(8,128)(2,1)S(1)}) custom-call(bf16[2,16,6784]{2,1,0:T(8,128)(2,1)S(1)} %pad_maximum_fusion.6.cat_in, f32[2,72,512]{2,1,0:T(8,128)S(1)} %maximum_convert_fusion.down_in), custom_call_target="tpu_custom_call" | custom-call | tf_op jit(solution)/shard_map/gather/pallas_call | solution.py:123
  116.4 2.1 copy-done
  119.7 4.1 %copy-done.1 = bf16[1024,6784]{1,0:T(8,128)(2,1)} copy-done((bf16[1024,6784]{1,0:T(8,128)(2,1)}, bf16[1024,6784]{1,0:T(8,128)(2,1)S(1)}, u32[]{:S(2)}) %copy-start.1) | copy-done | bytes 13893656
  124.9 1.9 constant_dynamic-slice_fusion.5
  129.0 4.1 %fusion.11 = f32[512,1536]{1,0:T(8,128)S(1)} fusion(bf16[1024,6784]{1,0:T(8,128)(2,1)} %copy-done.1, f32[1024]{0:T(1024)S(1)} %get-tuple-element.60, f32[512]{0:T(512)S(1)} %add_rsqrt_fusion, bf16[256,1024]{1,0:T(8,128)(2,1)} %collective-permute-done, bf16[256,1024]{1,0:T(8,128)(2,1)S(1)} %copy-done.6, pred[]{:T(512)S(6)} %eq.18), kind=kOutput, calls=%fused_computation.21 | convolution fusion | flops 1617428480 | bytes 7346177 | tf_op jit(solution)/shard_map/dot_general | solution.py:327
  136.8 3.1 collective-permute-start.1
  140.6 4.0 multiply_convert_fusion.8
  149.9 2.0 fusion.28
  151.9 2.0 constant_dynamic-slice_fusion.3
  156.7 6.7 %fusion.29 = f32[512,2304]{1,0:T(8,128)} fusion(bf16[2304,512]{1,0:T(8,128)(2,1)S(1)} %get-tuple-element.19, bf16[2304,512]{1,0:T(8,128)(2,1)S(1)} %constant_dynamic-slice_fusion.3, pred[]{:T(512)S(6)} %eq.18, bf16[256,1024]{1,0:T(8,128)(2,1)} %collective-permute-done.5, bf16[256,1024]{1,0:T(8,128)(2,1)} %fusion.28), kind=kOutput, calls=%fused_computation.76 | convolution fusion | flops 2441871360 | bytes 10485761 | tf_op jit(solution)/shard_map/dot_general | solution.py:329
  163.5 4.9 %fusion.3 = f32[512,2304]{1,0:T(8,128)} fusion(bf16[1024,6784]{1,0:T(8,128)(2,1)S(1)} %bitcast.48, bf16[256,1024]{1,0:T(8,128)(2,1)S(1)} %collective-permute-done.3, bf16[256,1024]{1,0:T(8,128)(2,1)S(1)} %multiply_convert_fusion.7, pred[]{:T(512)S(6)} %eq.18), kind=kOutput, calls=%fused_computation.12 | convolution fusion | flops 2420637696 | bytes 10485761 | tf_op jit(solution)/shard_map/dot_general | solution.py:327
  168.4 8.5 %multiply_convert_fusion.1 = (bf16[512,2304]{1,0:T(8,128)(2,1)}, bf16[512,2304]{1,0:T(8,128)(2,1)S(1)}, bf16[512,2304]{1,0:T(8,128)(2,1)}) fusion(f32[512,2304]{1,0:T(8,128)} %fusion.29, f32[512,2304]{1,0:T(8,128)} %fusion.3, bf16[1024,6784]{1,0:T(8,128)(2,1)S(1)} %bitcast.48, bf16[256,1024]{1,0:T(8,128)(2,1)S(1)} %collective-permute-done.3, ...), kind=kOutput, calls=%fused_computation.6 | convolution fusion | flops 2438332416 | bytes 22282240 | tf_op jit(solution)/shard_map/dot_general | solution.py:327
  176.9 2.6 fusion.1
  179.6 2.6 fusion.16
  183.3 2.8 fusion.30
  188.2 4.6 %convolution_convert_fusion = bf16[2304,1024]{1,0:T(8,128)(2,1)S(1)} fusion(bf16[512,2304]{1,0:T(8,128)(2,1)S(1)} %copy-done.26, bf16[256,1024]{1,0:T(8,128)(2,1)} %collective-permute-done.5, bf16[256,1024]{1,0:T(8,128)(2,1)} %fusion.28, pred[]{:T(512)S(6)} %eq.18), kind=kOutput, calls=%fused_computation | convolution fusion | flops 2422996992 | bytes 8126465 | tf_op jit(solution)/shard_map/dot_general | solution.py:328
  193.2 6.1 %convolution_convert_fusion.2 = bf16[1024,2304]{1,0:T(8,128)(2,1)} fusion(bf16[512,2304]{1,0:T(8,128)(2,1)} %get-tuple-element.77, bf16[256,1024]{1,0:T(8,128)(2,1)S(1)} %collective-permute-done.3, bf16[256,1024]{1,0:T(8,128)(2,1)S(1)} %multiply_convert_fusion.7, pred[]{:T(512)S(6)} %eq.18), kind=kOutput, calls=%fused_computation.2 | convolution fusion | flops 2422996992 | bytes 8126465 | tf_op jit(solution)/shard_map/dot_general | solution.py:328
  202.8 2.6 pad_maximum_fusion.gd
  205.5 6.3 %convolution_convert_fusion.1 = bf16[1024,2304]{1,0:T(8,128)(2,1)} fusion(bf16[512,2304]{1,0:T(8,128)(2,1)} %copy-done.24, bf16[256,1024]{1,0:T(8,128)(2,1)S(1)} %copy-done.22, bf16[256,1024]{1,0:T(8,128)(2,1)S(1)} %multiply_convert_fusion.7, pred[]{:T(512)S(6)} %eq.18), kind=kOutput, calls=%fused_computation.1 | convolution fusion | flops 2422996992 | bytes 8126465 | tf_op jit(solution)/shard_map/dot_general | solution.py:328
  211.8 2.3 multiply_reduce_fusion.2
  216.2 4.7 %collective-permute-done.8 = f32[2,512]{1,0:T(2,128)S(1)} collective-permute-done((f32[2,512]{1,0:T(2,128)S(1)}, f32[2,512]{1,0:T(2,128)S(1)}, u32[]{:S(2)}, u32[]{:S(2)}) %collective-permute-start.8) | collective-permute-done | bytes 4128 | tf_op jit(solution)/shard_map/ppermute | solution.py:387
  225.0 2.0 convolution_convert_fusion.4
  228.2 4.9 %convolution_convert_fusion.3 = bf16[1024,1536]{1,0:T(8,128)(2,1)} fusion(bf16[512,512]{1,0:T(8,128)(2,1)S(1)} %get-tuple-element.83, bf16[512,512]{1,0:T(8,128)(2,1)S(1)} %get-tuple-element.87, bf16[512,512]{1,0:T(8,128)(2,1)S(1)} %get-tuple-element.82, f32[1024]{0:T(1024)S(1)} %get-tuple-element.60, f32[512]{0:T(512)S(1)} %add_rsqrt_fusion, ...), kind=kOutput, calls=%fused_computation.18 | convolution fusion | flops 1623719936 | bytes 5773313 | tf_op jit(solution)/shard_map/dot_general | solution.py:328
  234.5 154.7 %scatter.1 = (f32[2,16,6784]{2,1,0:T(8,128)}, f32[2,72,512]{2,1,0:T(8,128)}) custom-call(bf16[4,4,64,1536]{3,2,1,0:T(8,128)(2,1)} %bitcast.53, bf16[2,2,4,64,512]{4,3,2,1,0:T(8,128)(2,1)} %pad_maximum_fusion.3.gout, bf16[4,4,64,128]{3,2,1,0:T(8,128)(2,1)} %bitcast.56, bf16[4,4,64,2304]{3,2,1,0:T(8,128)(2,1)} %bitcast.51, bf16[4,4,64,2304]{3,2,1,0:T(8,128)(2,1)} %bitcast.52, ...), custom_call_target="tpu_custom_call" | custom-call | tf_op jit(solution)/shard_map/scatter/pallas_call | solution.py:284
  (158 shorter events, 55.0 us)
Async XLA Ops:
  0.6 126.6 %collective-permute-start = (bf16[256,1024]{1,0:T(8,128)(2,1)}, bf16[256,1024]{1,0:T(8,128)(2,1)}, u32[]{:S(2)}, u32[]{:S(2)}) collective-permute-start(bf16[256,1024]{1,0:T(8,128)(2,1)} %param.11), channel_id=1, source_target_pairs={{0,1},{1,0},{2,3},{3,2},{4,5},{5,4},{6,7},{7,6},{8,9},{9,8},{10,11... | collective-permute-start | bytes 1572872 | tf_op jit(solution)/shard_map/ppermute | solution.py:312
  118.5 5.3 %copy-start.1 = (bf16[1024,6784]{1,0:T(8,128)(2,1)}, bf16[1024,6784]{1,0:T(8,128)(2,1)S(1)}, u32[]{:S(2)}) copy-start(bf16[1024,6784]{1,0:T(8,128)(2,1)S(1)} %get-tuple-element.16) | copy-start | bytes 41680900
  118.5 5.4 %copy-start.2 = (bf16[512,512]{1,0:T(8,128)(2,1)}, bf16[512,512]{1,0:T(8,128)(2,1)S(1)}, u32[]{:S(2)}) copy-start(bf16[512,512]{1,0:T(8,128)(2,1)S(1)} %get-tuple-element.17) | copy-start | bytes 1572868
  134.8 5.1 %copy-start.8 = (f32[3,1024]{0,1:T(8,128)S(1)}, f32[3,1024]{0,1:T(8,128)}, u32[]{:S(2)}) copy-start(f32[3,1024]{0,1:T(8,128)} %slice.251) | copy-start | bytes 36868
  136.0 8.6 %copy-start.3 = (bf16[512,512]{1,0:T(8,128)(2,1)S(1)}, bf16[512,512]{1,0:T(8,128)(2,1)}, u32[]{:S(2)}) copy-start(bf16[512,512]{1,0:T(8,128)(2,1)} %copy-done.2) | copy-start | bytes 1572868
  136.8 3.8 collective-permute-start.1
  147.8 6.1 %collective-permute-start.2 = (f32[256,1024]{1,0:T(8,128)}, f32[256,1024]{1,0:T(8,128)}, u32[]{:S(2)}, u32[]{:S(2)}) collective-permute-start(f32[256,1024]{1,0:T(8,128)} %constant_dynamic-slice_fusion.4), channel_id=1, source_target_pairs={{0,1},{1,0},{2,3},{3,2},{4,5},{5,4},{6,7},{7,6},{8,9},{9,8},{10,11... | collective-permute-start | bytes 3145736 | tf_op jit(solution)/shard_map/ppermute | solution.py:312
  151.9 4.8 %collective-permute-start.5 = (bf16[256,1024]{1,0:T(8,128)(2,1)}, bf16[256,1024]{1,0:T(8,128)(2,1)}, u32[]{:S(2)}, u32[]{:S(2)}) collective-permute-start(bf16[256,1024]{1,0:T(8,128)(2,1)} %fusion.28), channel_id=1, source_target_pairs={{0,1},{1,0},{2,3},{3,2},{4,5},{5,4},{6,7},{7,6},{8,9},{9,8},{10,11... | collective-permute-start | bytes 1572872 | tf_op jit(solution)/shard_map/ppermute | solution.py:312
  155.8 7.7 %slice-start = ((s8[13893632]{0:T(1024)(128)(4,1)}), s8[4194304]{0:T(1024)(128)(4,1)S(1)}, s32[]{:S(2)}) async-start(s8[13893632]{0:T(1024)(128)(4,1)} %bitcast.47), calls=%async_computation | async-start | bytes 8388608
  155.9 7.5 %collective-permute-start.3 = (bf16[256,1024]{1,0:T(8,128)(2,1)S(1)}, bf16[256,1024]{1,0:T(8,128)(2,1)S(1)}, u32[]{:S(2)}, u32[]{:S(2)}) collective-permute-start(bf16[256,1024]{1,0:T(8,128)(2,1)S(1)} %multiply_convert_fusion.7), channel_id=1, source_target_pairs={{0,1},{1,0},{2,3},{3,2},{4,5},{5,4},{6,7},{7,6},{8,9},{9,8},{10,11... | collective-permute-start | bytes 1572872 | tf_op jit(solution)/shard_map/ppermute | solution.py:312
  156.7 6.7 %slice-start.1 = ((s8[13893632]{0:T(1024)(128)(4,1)}), s8[4194304]{0:T(1024)(128)(4,1)S(1)}, s32[]{:S(2)}) async-start(s8[13893632]{0:T(1024)(128)(4,1)} %bitcast.47), calls=%async_computation.1 | async-start | bytes 8388608
  156.7 6.8 %slice-start.2 = ((s8[13893632]{0:T(1024)(128)(4,1)}), s8[4194304]{0:T(1024)(128)(4,1)S(1)}, s32[]{:S(2)}) async-start(s8[13893632]{0:T(1024)(128)(4,1)} %bitcast.47), calls=%async_computation.2 | async-start | bytes 8388608
  156.7 6.8 %slice-start.3 = ((s8[13893632]{0:T(1024)(128)(4,1)}), s8[1310720]{0:T(1024)(128)(4,1)S(1)}, s32[]{:S(2)}) async-start(s8[13893632]{0:T(1024)(128)(4,1)} %bitcast.47), calls=%async_computation.3 | async-start | bytes 2621440
  163.5 29.7 %copy-start.21 = (bf16[256,1024]{1,0:T(8,128)(2,1)}, bf16[256,1024]{1,0:T(8,128)(2,1)S(1)}, u32[]{:S(2)}) copy-start(bf16[256,1024]{1,0:T(8,128)(2,1)S(1)} %collective-permute-done.3) | copy-start | bytes 1572868
  183.3 15.9 %collective-permute-start.6 = (f32[256,1024]{1,0:T(8,128)}, f32[256,1024]{1,0:T(8,128)}, u32[]{:S(2)}, u32[]{:S(2)}) collective-permute-start(f32[256,1024]{1,0:T(8,128)} %constant_dynamic-slice_fusion.1), channel_id=1, source_target_pairs={{0,1},{1,0},{2,3},{3,2},{4,5},{5,4},{6,7},{7,6},{8,9},{9,8},{10,11... | collective-permute-start | bytes 3145736 | tf_op jit(solution)/shard_map/ppermute | solution.py:312
  187.5 13.5 %collective-permute-start.4 = (f32[256,1024]{1,0:T(8,128)S(1)}, f32[256,1024]{1,0:T(8,128)S(1)}, u32[]{:S(2)}, u32[]{:S(2)}) collective-permute-start(f32[256,1024]{1,0:T(8,128)S(1)} %constant_dynamic-slice_fusion.2), channel_id=1, source_target_pairs={{0,1},{1,0},{2,3},{3,2},{4,5},{5,4},{6,7},{7,6},{8,9},{9,8},{10,11... | collective-permute-start | bytes 3145736 | tf_op jit(solution)/shard_map/ppermute | solution.py:312
  202.8 8.9 %collective-permute-start.7 = (bf16[256,1024]{1,0:T(8,128)(2,1)}, bf16[256,1024]{1,0:T(8,128)(2,1)S(1)}, u32[]{:S(2)}, u32[]{:S(2)}) collective-permute-start(bf16[256,1024]{1,0:T(8,128)(2,1)} %get-tuple-element.68), channel_id=1, source_target_pairs={{0,1},{1,0},{2,3},{3,2},{4,5},{5,4},{6,7},{7,6},{8,9},{9,8},{10,11... | collective-permute-start | bytes 1572872 | tf_op jit(solution)/shard_map/ppermute | solution.py:312
  205.4 6.3 %copy-start.5 = (f32[512,1536]{1,0:T(8,128)S(1)}, f32[512,1536]{1,0:T(8,128)}, u32[]{:S(2)}) copy-start(f32[512,1536]{1,0:T(8,128)} %copy-done.4) | copy-start | bytes 9437188
  205.4 6.3 %copy-start.7 = (f32[512,512]{1,0:T(8,128)S(1)}, f32[512,512]{1,0:T(8,128)}, u32[]{:S(2)}) copy-start(f32[512,512]{1,0:T(8,128)} %get-tuple-element.75) | copy-start | bytes 3145732
  205.4 6.3 %copy-start.14 = (f32[512,512]{1,0:T(8,128)S(1)}, f32[512,512]{1,0:T(8,128)}, u32[]{:S(2)}) copy-start(f32[512,512]{1,0:T(8,128)} %get-tuple-element.74) | copy-start | bytes 3145732
  205.4 6.3 %copy-start.16 = (bf16[512,512]{1,0:T(8,128)(2,1)S(1)}, bf16[512,512]{1,0:T(8,128)(2,1)}, u32[]{:S(2)}) copy-start(bf16[512,512]{1,0:T(8,128)(2,1)} %copy-done.15) | copy-start | bytes 1572868
  205.5 6.3 %copy-start.20 = (bf16[512,512]{1,0:T(8,128)(2,1)S(1)}, bf16[512,512]{1,0:T(8,128)(2,1)}, u32[]{:S(2)}) copy-start(bf16[512,512]{1,0:T(8,128)(2,1)} %constant_dynamic-slice_fusion.5) | copy-start | bytes 1572868
  214.5 6.4 %collective-permute-start.8 = (f32[2,512]{1,0:T(2,128)S(1)}, f32[2,512]{1,0:T(2,128)S(1)}, u32[]{:S(2)}, u32[]{:S(2)}) collective-permute-start(f32[2,512]{1,0:T(2,128)S(1)} %add_multiply_fusion), channel_id=1, source_target_pairs={{2,0},{3,1},{4,2},{5,3},{6,4},{7,5},{8,6},{9,7},{10,8},{11,9},{12,... | collective-permute-start | bytes 12296 | tf_op jit(solution)/shard_map/ppermute | solution.py:387
  223.3 9.8 %collective-permute-start.9 = (f32[256,1024]{1,0:T(8,128)S(1)}, f32[256,1024]{1,0:T(8,128)S(1)}, u32[]{:S(2)}, u32[]{:S(2)}) collective-permute-start(f32[256,1024]{1,0:T(8,128)S(1)} %constant_dynamic-slice_fusion), channel_id=1, source_target_pairs={{0,1},{1,0},{2,3},{3,2},{4,5},{5,4},{6,7},{7,6},{8,9},{9,8},{10,11... | collective-permute-start | bytes 3145736 | tf_op jit(solution)/shard_map/ppermute | solution.py:312
  (17 other events, 41.4 us)

commit v2 on v0

v2 whole, which is shorter than its diff:
```python
import functools
import jax, jax.numpy as jnp
from jax import lax
from jax.experimental import pallas as pl
from jax.experimental.pallas import tpu as pltpu
from jax.sharding import PartitionSpec as P
MESH = pl.DeviceIdType.MESH
EPS = 1e-05
bf, f32 = jnp.bfloat16, jnp.float32
C1 = 2176; HALF = 1152; CAT = 6784; UNIT = 32; DUNIT = 144; FH = 2304
COPIES = 272
JS = (2, -1, 1, 0)
PAIR, CROSS, X, Y = 1, 2, 0, 1
ONE, TWO, THREE = 1, 2, 3
XY, YX = (X, Y), (Y, X)
class Box:
    def __init__(self, *a, **kw):
        for d in a: self.__dict__.update(d)
        self.__dict__.update(kw)

FLOWS = Box(
    f1a=Box(kind=1, base=0, step=512, gw=512, fw=512, to=PAIR, order=XY),
    f1b=Box(kind=1, base=1024, step=384, gw=768, fw=384, to=CROSS, order=YX),
    f2a=Box(kind=2, base=C1, step=768, gw=1536, fw=768, to=PAIR, order=YX),
    f2b=Box(kind=2, base=C1 + FH, step=640, gw=1664, fw=640, to=CROSS, order=XY),
    f3a=Box(kind=3, base=0, step=0, gw=256, fw=0, to=None, order=XY),
    f3b=Box(kind=3, base=256, step=0, gw=256, fw=0, to=None, order=YX))

def spot():
    rep = lax.axis_index("rep"); s = lax.axis_index("shard")
    return (s // 4) % 4, s // 16, ((s // 2) % 2) * 2 + rep, s % 2

def device(x, y, z, c):
    return (z % 2, ((y * 4 + x) * 2 + z // 2) * 2 + c)

def moved(x, y, z, c, axis, step):
    if axis == X: return device((x + step + 4) % 4, y, z, c)
    return device(x, (y + step + 4) % 4, z, c)

def along(x, y, z, c, step):
    k = ((y * 4 + x) * 2 + z // 2 + step + 32) % 32
    return device((k // 2) % 4, k // 8, (k % 2) * 2 + z % 2, c)

def greet(devices):
    bar = pltpu.get_barrier_semaphore()
    for d in devices:
        pl.semaphore_signal(bar, inc=1, device_id=d, device_id_type=MESH)
    pl.semaphore_wait(bar, len(devices))

class Copy:
    def __init__(self, cp): self.cp, self.here, self.gone = cp, False, False
    def wait_recv(self): self.cp.wait_recv(); self.here = True
    def wait_send(self): self.cp.wait_send(); self.gone = True

class Wire:
    def __init__(self, ss, rs, ls): self.ss, self.rs, self.ls, self.sent, self.n = ss, rs, ls, [], 0
    def send(self, src, dst, dev):
        i = len(self.sent)
        cp = pltpu.make_async_remote_copy(src_ref=src, dst_ref=dst, send_sem=self.ss.at[i], recv_sem=self.rs.at[i], device_id=dev, device_id_type=MESH)
        cp.start(); self.sent.append(Copy(cp)); return self.sent[-1]
    def local(self, src, dst):
        cp = pltpu.make_async_copy(src, dst, self.ls.at[self.n]); self.n += 1; cp.start(); return cp
    def drain(self):
        for cp in self.sent:
            if not cp.here: cp.wait_recv()
            if not cp.gone: cp.wait_send()

def at_rows(v, n, m=16): return pl.ds(pl.multiple_of(v, m), n)

class Pump:
    def __init__(self, steps): self.steps, self.seen = steps, set()
    def run(self, n):
        for _ in range(n):
            t = next(self.steps, None)
            if t is None: return False
            self.seen.add(t)
        return True
    def until(self, tag):
        while tag not in self.seen:
            if not self.run(1): raise ValueError(tag)
    def finish(self):
        while self.run(1): pass

def gather_steps(w, go, pair, cross, other, x, y, z, wcat, wd, wdr, dnb, k, unit_in, unit_down):
    hi = z // 2
    urow = at_rows(UNIT * k, UNIT, UNIT)
    drow = at_rows(DUNIT * k, DUNIT)
    cat = lambda a, n: wcat.at[urow, pl.ds(a, n)]
    unit_in()
    z1 = w.send(cat(0, C1), cat(0, C1), cross)
    z2 = w.send(cat(C1, CAT - C1), cat(C1, CAT - C1), cross)
    unit_down()
    z3 = w.send(dnb, wd.at[drow, :], cross)
    ldb = w.local(dnb, wd.at[drow, :])
    def F(t, need):
        sel = {PAIR: z % 2, CROSS: hi, None: 0}[t.to]
        d = t.kind == 3
        return Box(vars(t), buf=wd if d else wcat, unit=DUNIT if d else UNIT, mine=(t.base + t.step * sel, t.gw), alone=(t.base + t.gw * sel, t.fw),
            need=need, fwd={PAIR: pair, CROSS: cross, None: None}[t.to], z=[], p={}, m={}, p2={}, m2={})
    p1 = [F(FLOWS.f1a, [z1.wait_recv]), F(FLOWS.f1b, [])]
    p2 = [F(FLOWS.f2a, [z2.wait_recv]), F(FLOWS.f2b, [])]
    p3 = [F(FLOWS.f3a, [z3.wait_recv, ldb.wait]), F(FLOWS.f3b, [])]
    def block(f, da, db, unit=None, cols=None, buf=None):
        a, b = f.order
        pos = {X: x, Y: y}
        pos[a] = (pos[a] + da + 4) % 4
        pos[b] = (pos[b] + db + 4) % 4
        u = f.unit
        row = (pos[Y] * 4 + pos[X]) * (2 * u)
        n = 2 * u
        if unit is not None: row, n = row + unit * u, u
        col, width = cols or f.mine
        return (f.buf if buf is None else buf).at[at_rows(row, n), pl.ds(col if isinstance(col, int) else pl.multiple_of(col, 128), width)]
    def push(f, da, db, dev, unit=None):
        v = block(f, da, db, unit)
        return w.send(v, v, dev)
    def fwd(f, da, db):
        if f.fwd is not None:
            v = block(f, da, db, None, f.alone)
            f.z.append(w.send(v, v, f.fwd))
        if f.kind == 3:
            v = block(f, da, db)
            f.z.append(w.send(v, block(f, da, db, None, f.mine, wdr), other))
    def open2(f, j):
        b = f.order[1]
        f.p[j] = push(f, j, 0, go[(b, 1)])
        f.m[j] = push(f, j, 0, go[(b, -1)])
    def r1(f):
        for q in f.need: q()
        a = f.order[0]
        f.p[None] = push(f, 0, 0, go[(a, 1)])
        f.m[None] = push(f, 0, 0, go[(a, -1)])
        open2(f, 0)
        if f.kind == 3: fwd(f, 0, 0)
    def r2(f):
        a = f.order[0]
        f.p[None].wait_recv(); f.p2[None] = push(f, -1, 0, go[(a, 1)], 0)
        f.m[None].wait_recv(); f.m2[None] = push(f, 1, 0, go[(a, -1)], 1)
        open2(f, -1); open2(f, 1)
        fwd(f, -1, 0); fwd(f, 1, 0)
    def r3(f):
        f.p2[None].wait_recv(); f.m2[None].wait_recv()
        open2(f, 2); fwd(f, 2, 0)
    def r4(f, j):
        b = f.order[1]
        f.p[j].wait_recv(); f.p2[j] = push(f, j, -1, go[(b, 1)], 0)
        f.m[j].wait_recv(); f.m2[j] = push(f, j, 1, go[(b, -1)], 1)
        fwd(f, j, -1); fwd(f, j, 1)
    def r5(f, j):
        f.p2[j].wait_recv(); f.m2[j].wait_recv()
        fwd(f, j, 2)
    def both(g, p, *a):
        for f in p: g(f, *a)
    order = (0, -1, 1, 2)
    both(r1, p1); yield 0
    both(r2, p1); yield 0
    both(r3, p1); yield 0
    both(r1, p2); yield 0
    both(r4, p1, 0); yield 0
    both(r4, p1, -1); yield 0
    both(r4, p1, 1); yield 0
    both(r2, p2); yield 0
    both(r4, p1, 2); yield 0
    both(r3, p2); yield 0
    for j in order: both(r5, p1, j)
    for f in p1:
        for q in f.z: q.wait_recv()
    yield ONE
    both(r4, p2, 0); yield 0
    both(r1, p3); yield 0
    both(r4, p2, -1); yield 0
    both(r4, p2, 1); yield 0
    both(r2, p3); yield 0
    both(r4, p2, 2); yield 0
    both(r3, p3); yield 0
    both(r5, p2, 0); both(r5, p2, -1); yield 0
    both(r4, p3, 0); yield 0
    both(r5, p2, 1); both(r5, p2, 2); yield 0
    both(r4, p3, -1); yield 0
    for f in p2:
        for q in f.z: q.wait_recv()
    yield TWO
    both(r4, p3, 1); yield 0
    both(r4, p3, 2); yield 0
    for j in order: both(r5, p3, j)
    yield THREE

def dot(a, b): return jnp.dot(a, b, preferred_element_type=f32)
def tn(a, b): return lax.dot_general(a, b, (((0,), (0,)), ((), ())), preferred_element_type=f32)
def nt(a, b): return lax.dot_general(a, b, (((1,), (1,)), ((), ())), preferred_element_type=f32)

A_GOT = dict(wcat=((1024, CAT), bf), wd=((4608, 512), bf), wor=((512, 512), bf), wdr=((4608, 512), bf))
A_MADE = dict(h=((512, 1024), bf), bcx=((512, 1536), bf), ext=((528, 512), f32), conv=((512, 512), bf), y=((512, 512), bf),
    resid=((256, 1024), f32), h2=((512, 1024), bf), gate=((512, FH), bf), up=((512, FH), bf), act=((512, FH), bf),
    dffo=((512, 1024), bf), ddown=((2, FH, 512), bf), small=((8, 1024), f32))
A_SCR = dict(T=((512, 1024), bf), cotv=((256, 1024), bf), win=((1024, 1536), bf), wo=((512, 1024), bf), wsm=((1024, 128), bf),
    wg=((1024, FH), bf), wu=((1024, FH), bf), cpart=((512, 512), f32), mixs=((256, 1024), f32), mixr=((256, 1024), f32),
    dnf=((DUNIT, 512), f32), dns=((72, 512), f32), dnb=((DUNIT, 512), bf),
    inp=((16, 3072), bf), outp=((16, 1024), bf), sml=((16, 128), bf), wgs=((16, 4608), bf), wus=((16, 4608), bf), wds=((72, 1024), bf), keepv=((256, 1), f32))

def named(groups, refs):
    refs, out = list(refs), []
    for g in groups:
        out.append(Box(dict(zip(g, refs)))); refs = refs[len(g):]
    return out, refs

def forward_kernel(*refs):
    A_IN = dict(tokens=0, cot=0, keep=0, inp=0, outp=0, sml=0, wgs=0, wus=0, wds=0)
    (I, O, M, V, S), (ss, rs, ls) = named([A_IN, A_GOT, A_MADE, A_MADE, A_SCR], refs)
    wcat, wd, wor, wdr = O.wcat, O.wd, O.wor, O.wdr
    x, y, z, c = spot()
    hi = z // 2
    s = ((y * 4 + x) * 2 + hi) * 2 + c
    k = s // 2
    pair = device(x, y, z + 1 - 2 * (z % 2), c)
    cross = device(x, y, 3 - z, c)
    other = device(x, y, z, 1 - c)
    nxt, prv = along(x, y, z, c, 1), along(x, y, z, c, -1)
    go = {(a, st): moved(x, y, z, c, a, st) for a in XY for st in (1, -1)}
    w = Wire(ss, rs, ls)
    own, oth = at_rows(256 * c, 256, 256), at_rows(256 * (1 - c), 256, 256)
    col = lambda p, n: pl.ds(pl.multiple_of(p, 128), n)
    lds = w.local(I.wds, S.wds)
    lin = [w.local(a, b) for a, b in ((I.sml, S.sml), (I.inp, S.inp), (I.outp, S.outp), (I.wgs, S.wgs), (I.wus, S.wus))]
    lcot = [w.local(I.cot, S.cotv), w.local(I.keep, S.keepv)]
    ltok = w.local(I.tokens, S.T.at[own])
    greet(list(go.values()) + [pair, cross, other, nxt, prv])
    rows = at_rows(16 * s, 16)
    pieces = [(I.inp, S.inp, 1024 * i, 512, 512 * i) for i in range(3)] + [(I.outp, S.outp, 0, 512, 1536), (I.wgs, S.wgs, 0, FH, C1), (I.wus, S.wus, 0, FH, C1 + FH)]
    got = [w.send(I.sml, wcat.at[rows, pl.ds(2048, 128)], other)]
    for src, _, a, n, d in pieces: got.append(w.send(src.at[:, col(a + n * (1 - c), n)], wcat.at[rows, pl.ds(d, n)], other))
    for q in lin: q.wait()
    mine = [w.local(S.sml, wcat.at[rows, pl.ds(2048, 128)])]
    for _, src, a, n, d in pieces: mine.append(w.local(src.at[:, col(a + n * c, n)], wcat.at[rows, pl.ds(d, n)]))
    lds.wait()
    S.dns[...] = S.wds[:, col(512 * (1 - c), 512)].astype(f32)
    gdn = w.send(S.dns, S.dnf.at[at_rows(72 * c, 72, 8)], other)
    S.dnf[at_rows(72 * c, 72, 8), :] = S.wds[:, col(512 * c, 512)].astype(f32)
    gtok = w.send(I.tokens, S.T.at[own], other)
    def unit_in():
        for q in mine: q.wait()
        for q in got: q.wait_recv()
    def unit_down():
        gdn.wait_recv()
        S.dnb[...] = S.dnf[...].astype(bf)
    pump = Pump(gather_steps(w, go, pair, cross, other, x, y, z, wcat, wd, wdr, S.dnb, k, unit_in, unit_down))
    pump.run(1)
    for q in lcot: q.wait()
    V.dffo[own, :] = (S.keepv[...] * S.cotv[...].astype(f32)).astype(bf)
    gdf = w.send(V.dffo.at[own], V.dffo.at[own], other)
    ltok.wait(); gtok.wait_recv()
    outs = []
    def save(**kw):
        for n in kw: outs.append(w.local(vars(V)[n], vars(M)[n]))
    pump.until(ONE)
    l1 = w.local(wcat.at[:, pl.ds(2048, 128)], S.wsm)
    l2 = w.local(wcat.at[:, pl.ds(0, 1536)], S.win)
    go_ = w.send(wcat.at[at_rows(512 * (1 - c), 512, 512), pl.ds(1536, 512)], wor, other)
    l3 = w.local(wcat.at[at_rows(512 * c, 512, 512), pl.ds(1536, 512)], S.wo.at[:, col(512 * c, 512)])
    l1.wait()
    eye = (lax.broadcasted_iota(jnp.int32, (8, 128), 0) == lax.broadcasted_iota(jnp.int32, (8, 128), 1)).astype(f32).astype(bf)
    V.small[...] = nt(eye, S.wsm[...])
    g1, g2 = V.small[0:1, :], V.small[1:2, :]
    def norm1(i, _):
        q = at_rows(i * 64, 64, 64)
        t = S.T[q, :].astype(f32)
        sc = lax.rsqrt(jnp.mean(t * t, axis=1, keepdims=True) + EPS)
        V.h[q, :] = (t * sc * g1).astype(bf)
        return 0
    lax.fori_loop(0, 8, norm1, 0)
    l2.wait(); go_.wait_recv()
    l4 = w.local(wor, S.wo.at[:, col(512 * (1 - c), 512)])
    ext = V.ext
    for n in (0, 256):
        b_ = dot(V.h[...], S.win[:, n:n + 256])
        x_ = dot(V.h[...], S.win[:, 1024 + n:1280 + n])
        V.bcx[:, n:n + 256] = b_.astype(bf)
        V.bcx[:, 1024 + n:1280 + n] = x_.astype(bf)
        ext[16:528, n:n + 256] = (b_ * x_).astype(bf).astype(f32)
    ghalo = w.send(ext.at[pl.ds(520, 8)], ext.at[pl.ds(8, 8)], nxt)
    pump.run(1)
    for n in (0, 256):
        c_ = dot(V.h[...], S.win[:, 512 + n:768 + n])
        S.cpart[:, n:n + 256] = c_
        V.bcx[:, 512 + n:768 + n] = c_.astype(bf)
    l3.wait(); l4.wait()
    ghalo.wait_recv()
    inside = (k > 0).astype(f32)
    ext[8:16, :] = ext[8:16, :] * inside
    t0, t1, t2 = (V.small[2 + i:3 + i, col(512 * c, 512)] for i in range(3))
    for q in range(0, 512, 128):
        cv = t0 * ext[14 + q:142 + q, :] + t1 * ext[15 + q:143 + q, :] + t2 * ext[16 + q:144 + q, :]
        V.conv[q:q + 128, :] = cv.astype(bf)
        V.y[q:q + 128, :] = (S.cpart[q:q + 128, :] * cv).astype(bf)
    S.mixs[...] = dot(V.y[oth, :], S.wo[...])
    gmix = w.send(S.mixs, S.mixr, other)
    V.resid[...] = dot(V.y[own, :], S.wo[...])
    save(h=1, bcx=1, ext=1, conv=1, y=1, small=1)
    pump.run(1)
    gmix.wait_recv()
    def norm2(i, _):
        q = at_rows(i * 64, 64, 64)
        t = S.T[at_rows(256 * c + i * 64, 64, 64), :].astype(f32) + (V.resid[q, :] + S.mixr[q, :])
        V.resid[q, :] = t
        sc = lax.rsqrt(jnp.mean(t * t, axis=1, keepdims=True) + EPS)
        V.h2[at_rows(256 * c + i * 64, 64, 64), :] = (t * sc * g2).astype(bf)
        return 0
    lax.fori_loop(0, 4, norm2, 0)
    gh2 = w.send(V.h2.at[own], V.h2.at[own], other)
    save(resid=1)
    pump.until(TWO)
    lg = w.local(wcat.at[:, pl.ds(C1, FH)], S.wg)
    lu = w.local(wcat.at[:, pl.ds(C1 + FH, FH)], S.wu)
    gh2.wait_recv(); gdf.wait_recv()
    save(h2=1, dffo=1)
    lg.wait(); lu.wait()
    for n in range(0, FH, 768):
        g_ = dot(V.h2[...], S.wg[:, n:n + 768])
        u_ = dot(V.h2[...], S.wu[:, n:n + 768])
        V.gate[:, n:n + 768] = g_.astype(bf)
        V.up[:, n:n + 768] = u_.astype(bf)
        V.act[:, n:n + 768] = (g_ * jax.nn.sigmoid(g_) * u_).astype(bf)
        pump.run(1)
    save(gate=1, up=1, act=1)
    def down(i, _):
        q = at_rows(i * 256, 256, 256)
        t = tn(V.act[:, q], V.dffo[...]).astype(bf)
        V.ddown[0, q, :] = t[:, :512]
        V.ddown[1, q, :] = t[:, 512:]
        return 0
    lax.fori_loop(0, 9, down, 0)
    save(ddown=1)
    pump.finish()
    for q in outs: q.wait()
    w.drain()

def call(kernel, outs, scratch, ident, limit, extra, *args):
    hbm = pl.BlockSpec(memory_space=pl.ANY)
    return pl.pallas_call(
        kernel, out_shape=tuple(jax.ShapeDtypeStruct(*v) for v in outs), in_specs=[hbm] * len(args), out_specs=(hbm,) * len(outs),
        scratch_shapes=[pltpu.VMEM(*v) for v in scratch] + [pltpu.SemaphoreType.DMA((n,)) for n in (COPIES, COPIES, 96)] + extra,
        compiler_params=pltpu.CompilerParams(collective_id=ident, has_side_effects=True, vmem_limit_bytes=limit * 2**20))(*args)

def forward_all(*args):
    outs = call(forward_kernel, [*A_GOT.values(), *A_MADE.values()], [*A_MADE.values(), *A_SCR.values()], 1, 60, [], *args)
    return dict(zip([*A_GOT, *A_MADE], outs))

def smalls(norm1_gain, norm2_gain, conv_weight):
    small = jnp.concatenate([norm1_gain[:, None], norm2_gain[:, None], conv_weight.T], axis=1)
    return jnp.pad(small, ((0, 0), (0, 123)))


RFLOWS = dict(
    f1a=Box(kind=1, base=0, step=0, gw=256, fw=0, to=None, order=XY),
    f1b=Box(kind=1, base=256, step=0, gw=256, fw=0, to=None, order=YX),
    f1s=Box(kind=0, base=0, step=0, gw=128, fw=0, to=None, order=XY),
    f2a=Box(kind=2, base=0, step=768, gw=1536, fw=768, to=PAIR, order=YX),
    f2b=Box(kind=2, base=FH, step=640, gw=1664, fw=640, to=CROSS, order=XY),
    f3a=Box(kind=3, base=0, step=128, gw=128, fw=128, to=PAIR, order=YX),
    f3b=Box(kind=3, base=256, step=128, gw=128, fw=128, to=CROSS, order=XY))
UNITS, WIDTH = (32, 128, 32, 144), (128, 512, 2 * FH, 512)
B_OUT = dict(mixed=((256, 1024), bf), dtok=((256, 1024), f32), din=((16, 3072), f32), dout=((16, 1024), f32),
    dg=((16, 4608), f32), du=((16, 4608), f32), dd=((72, 1024), f32), ds=((2, 16, 128), f32))
GRADS = [((4, 4, 2, u, n), bf) for u, n in zip(UNITS, WIDTH)]
def flow_scratch(t):
    u, both = UNITS[t.kind], t.gw + t.fw
    n = 2 if t.to == PAIR else 1
    return [((6, u, t.gw), bf), ((n, u, t.gw), bf), ((n, u, both), bf), ((u, both), bf), ((u, both), f32)]
B_SCR = dict(W=((2, FH, 512), bf), gate=((512, FH), bf), up=((512, FH), bf), dffo=((512, 1024), bf), h2=((512, 1024), bf),
    bcx=((512, 1536), bf), ext=((528, 512), f32), resid=((256, 1024), f32), small=((8, 1024), f32),
    tok=((256, 1024), bf), dhs=((256, 1024), f32), dhr=((256, 1024), f32), dho=((256, 1024), f32), dcv=((520, 512), f32),
    gsum=((8, 1024), f32), keep=((256, 1), f32))

def add_into(dst, srcs, rows, step=16):
    def body(i, _):
        r = pl.ds(pl.multiple_of(i * step, step), step)
        t = dst[r, :].astype(f32)
        for q in srcs: t = t + q[r, :].astype(f32)
        dst[r, :] = t.astype(bf)
        return 0
    lax.fori_loop(0, rows // step, body, 0)

class Scatter:
    def __init__(self, w, go, pair, cross, x, y, z, c, other, grads, lands, bufs):
        self.w, self.go, self.x, self.y, self.z, self.c, self.other = w, go, x, y, z, c, other
        self.hi, self.zl = z // 2, z % 2
        self.f = Box()
        for i, (n, t) in enumerate(RFLOWS.items()):
            sel = {PAIR: self.zl, CROSS: self.hi, None: 0}[t.to]
            k = t.kind
            f = Box(vars(t), G=grads[k], L=lands[k], u=UNITS[k], sel=sel, col=t.base + t.step * sel, out=[],
                ecol=t.base + t.gw * sel, pcol=t.base + t.gw * (1 - sel), dev={PAIR: pair, CROSS: cross, None: None}[t.to],
                A={}, s={}, t={}, s2={}, t2={})
            f.M, f.E, f.S, f.R, f.F = bufs[5 * i:5 * i + 5]
            vars(self.f)[n] = f
        self.pair, self.cross = pair, cross
    def cols(self, c, n): return pl.ds(c if isinstance(c, int) else pl.multiple_of(c, 128), n)
    def at(self, f, da, db):
        a, b = f.order
        pos = {X: self.x, Y: self.y}
        pos[a] = (pos[a] + da + 4) % 4
        pos[b] = (pos[b] + db + 4) % 4
        return pos[Y], pos[X]
    def part(self, ref, f, p, u=None):
        if u is None: return ref.at[p[0], p[1], :, :, self.cols(f.col, f.gw)]
        return ref.at[p[0], p[1], u, :, self.cols(f.col, f.gw)]
    def zline(self, ref, f, j, col):
        l = self.at(f, j, 0)
        cs = self.cols(col, f.fw)
        return ref.at[l[0], :, :, :, cs] if f.order[0] == Y else ref.at[:, l[1], :, :, cs]
    def zsend(self, f, j):
        f.A[j] = self.w.send(self.zline(f.G, f, j, f.pcol), self.zline(f.L, f, j, f.ecol), f.dev)
    def first(self, f, j):
        b = f.order[1]
        if f.to:
            f.A[j].wait_recv()
            g, l = self.zline(f.G, f, j, f.ecol), self.zline(f.L, f, j, f.pcol)
            for i in range(4):
                for u in (0, 1): add_into(g.at[i, u], [l.at[i, u]], f.u)
        p = self.at(f, j, 2)
        f.s[j] = self.w.send(self.part(f.G, f, p, 0), self.part(f.L, f, p, 0), self.go[(b, 1)])
        f.t[j] = self.w.send(self.part(f.G, f, p, 1), self.part(f.L, f, p, 1), self.go[(b, -1)])
    def second(self, f, j):
        b, u = f.order[1], f.u
        f.s[j].wait_recv(); p = self.at(f, j, 1)
        add_into(self.part(f.G, f, p, 0), [self.part(f.L, f, p, 0)], u)
        f.s2[j] = self.w.send(self.part(f.G, f, p), self.part(f.L, f, p), self.go[(b, 1)])
        f.t[j].wait_recv(); p = self.at(f, j, -1)
        add_into(self.part(f.G, f, p, 1), [self.part(f.L, f, p, 1)], u)
        f.t2[j] = self.w.send(self.part(f.G, f, p), self.part(f.L, f, self.at(f, j, 1)), self.go[(b, -1)])
    def third(self, f, j):
        a, u, M = f.order[0], f.u, f.M
        f.s2[j].wait_recv(); f.t2[j].wait_recv()
        p = self.at(f, j, 0); o = self.at(f, j, 2)
        for v in (0, 1): add_into(self.part(f.G, f, p, v), [self.part(f.L, f, p, v), self.part(f.L, f, o, v)], u)
        if j == 2:
            f.c = self.w.send(self.part(f.G, f, p, 0), M.at[0], self.go[(a, 1)])
            f.d = self.w.send(self.part(f.G, f, p, 1), M.at[1], self.go[(a, -1)])
        elif j == 1:
            f.c.wait_recv(); add_into(self.part(f.G, f, p, 0), [M.at[0]], u)
            f.c2 = self.w.send(self.part(f.G, f, p), M.at[pl.ds(2, 2)], self.go[(a, 1)])
        elif j == -1:
            f.d.wait_recv(); add_into(self.part(f.G, f, p, 1), [M.at[1]], u)
            f.d2 = self.w.send(self.part(f.G, f, p), M.at[pl.ds(4, 2)], self.go[(a, -1)])
    def last1(self, f):
        u, M, me = f.u, f.M, (self.y, self.x)
        f.c2.wait_recv(); f.d2.wait_recv()
        for v in (0, 1): add_into(self.part(f.G, f, me, v), [M.at[2 + v], M.at[4 + v]], u)
        if f.to == PAIR: f.e = self.w.send(self.part(f.G, f, me), f.E, self.pair)
        else: f.e = self.w.send(self.part(f.G, f, me, 1 - self.hi), f.E.at[0], self.cross)
    def last2(self, f):
        E, S, R = f.E, f.S, f.R
        f.e.wait_recv()
        gw, fw, sel, base = f.gw, f.fw, f.sel, f.base
        ov = gw - fw
        def merge(i, v):
            G = f.G.at[self.y, self.x, v]
            m = self.cols(fw * 0 + (gw * sel if fw else 0), fw) if fw else None
            if fw:
                S[i, :, self.cols(gw * sel, fw)] = G[:, self.cols(base + gw * sel, fw)]
                S[i, :, self.cols(gw * (1 - sel), fw)] = E[i, :, self.cols(ov * (1 - sel), fw)]
            if ov:
                S[i, :, pl.ds(fw, ov)] = (G[:, pl.ds(base + fw, ov)].astype(f32) + E[i, :, self.cols(fw * sel, ov)].astype(f32)).astype(bf)
        if f.to == PAIR:
            merge(0, 0); merge(1, 1)
            f.e2 = self.w.send(S.at[1 - self.hi], R, self.cross)
        else:
            merge(0, self.hi)
            f.e2 = self.w.send(S.at[0], R, self.pair)
    def last3(self, f, targets):
        S, R, F = f.S, f.R, f.F
        f.e2.wait_recv()
        i = self.hi if f.to == PAIR else 0
        F[...] = S[i].astype(f32) + R[...].astype(f32)
        rows = f.u if f.kind == 3 else 32
        half = rows // 2
        m = 8
        for prow, pcol, pw, out, ocol in targets:
            src = lambda q: F.at[pl.ds(pl.multiple_of(prow + half * q, m), half), pl.ds(pcol, pw)]
            dst = out if ocol is None else out.at[:, self.cols(ocol, pw)]
            f.out.append(self.w.send(src(1 - self.c), dst, self.other))
            f.out.append(self.w.local(src(self.c), dst))
    def wait_out(self, f):
        for i, q in enumerate(f.out):
            if i % 2: q.wait()
            else: q.wait_recv()

def backward_kernel(*refs):
    (I, O, r), refs = named([dict(A_GOT, **A_MADE, tokens=0, keep=0), B_OUT, B_SCR], refs)
    grads, lands, bufs, (ss, rs, ls, free) = refs[:4], refs[4:8], refs[8:-4], refs[-4:]
    x, y, z, c = spot()
    hi = z // 2
    k = (y * 4 + x) * 2 + hi
    pair = device(x, y, z + 1 - 2 * (z % 2), c)
    cross = device(x, y, 3 - z, c)
    other = device(x, y, z, 1 - c)
    nxt, prv = along(x, y, z, c, 1), along(x, y, z, c, -1)
    go = {(a, st): moved(x, y, z, c, a, st) for a in XY for st in (1, -1)}
    greet(list(go.values()) + [pair, cross, other, nxt, prv])
    w = Wire(ss, rs, ls)
    sc = Scatter(w, go, pair, cross, x, y, z, c, other, grads, lands, bufs)
    F = sc.f
    own, oth = at_rows(256 * c, 256, 256), at_rows(256 * (1 - c), 256, 256)
    col = lambda p, n: pl.ds(pl.multiple_of(p, 128), n)
    W = r.W
    slot = lambda i: W.at[i // 2, pl.ds(1024 * (i % 2), 1024)]
    rdd = w.send(I.ddown.at[1 - c], grads[3].at[pl.ds(2 * c, 2)], other)
    ldd = w.local(I.ddown.at[c], grads[3].at[pl.ds(2 * c, 2)])
    lw = [w.local(I.wd.at[at_rows(FH * c, FH, FH), :], W.at[c]), w.local(I.wdr.at[at_rows(FH * c, FH, FH), :], W.at[1 - c])]
    ld = Box({n: w.local(vars(I)[n], vars(r)[n]) for n in dict(dffo=0, gate=0, up=0, h2=0, small=0, resid=0, ext=0, bcx=0, keep=0)})
    ld.tok = w.local(I.tokens, r.tok)
    ldd.wait(); rdd.wait_recv()
    for j in JS:
        sc.zsend(F.f3a, j); sc.zsend(F.f3b, j)
    for q in lw: q.wait()
    for q in (ld.dffo, ld.gate, ld.up): q.wait()
    def d_act(n):
        t = nt(r.dffo[:, :512], W[0, n:n + 768, :]) + nt(r.dffo[:, 512:], W[1, n:n + 768, :])
        g, u = r.gate[:, n:n + 768].astype(f32), r.up[:, n:n + 768].astype(f32)
        sg = jax.nn.sigmoid(g)
        r.gate[:, n:n + 768] = (t * u * sg * (1.0 + g * (1.0 - sg))).astype(bf)
        r.up[:, n:n + 768] = (t * (g * sg)).astype(bf)
    for n in range(0, FH, 768): d_act(n)
    P3, P2, P1, P0 = (F.f3a, F.f3b), (F.f2a, F.f2b), (F.f1a, F.f1b), (F.f1s,)
    def do(fn, ns, *a):
        for n in ns: fn(n, *a)
    panels = [[(r.gate, C1 + 512 * p, 512, 512 * p)] for p in range(4)] + [[(r.up, C1 + FH + 512 * p, 512, 512 * p)] for p in range(4)]
    panels += [[(r.gate, C1 + 2048, 256, 2048), (r.up, C1 + FH + 2048, 256, 2048)]]
    def fetch(i):
        out, o = [], 0
        for _, cc, n, _ in panels[i]:
            out.append(w.local(I.wcat.at[:, pl.ds(cc, n)], slot(i % 4).at[:, pl.ds(o, n)])); o += n
        return out
    got = {i: fetch(i) for i in range(4)}
    ld.h2.wait()
    def slab(src, yy, base):
        t = tn(r.h2[:, col(256 * yy, 256)], src[...]).astype(bf)
        for xx in range(4):
            for u in (0, 1): grads[2][yy, xx, u, :, base:base + FH] = t[64 * xx + 32 * u:64 * xx + 32 * u + 32]
    for j in JS:
        slab(r.gate, (y + j + 4) % 4, 0)
        sc.zsend(F.f2a, j)
    do(sc.first, P3, 2)
    def slabs(i, _):
        slab(r.up, i, FH)
        return 0
    lax.fori_loop(0, 4, slabs, 0)
    for j in JS: sc.zsend(F.f2b, j)
    do(sc.first, P3, -1); do(sc.second, P3, 2)
    for i in range(9):
        for q in got[i]: q.wait()
        o = 0
        for nm, _, n, off in panels[i]:
            for rr, acc in ((oth, r.dhs), (own, r.dho)):
                t = nt(nm[rr, off:off + n], slot(i % 4)[:, o:o + n])
                acc[...] = t if i == 0 else acc[...] + t
            o += n
        if i + 4 < 9: got[i + 4] = fetch(i + 4)
        if i == 4: do(sc.first, P3, 1)
    gdh = w.send(r.dhs, r.dhr, other)
    r.h, r.y, r.conv = (r.gate.at[:, pl.ds(o, m)] for o, m in ((0, 1024), (1024, 512), (1536, 512)))
    ld.h, ld.y, ld.conv = w.local(I.h, r.h), w.local(I.y, r.y), w.local(I.conv, r.conv)
    lin = [w.local(I.wcat.at[:, pl.ds(512 * i, 512)], slot(i + 1)) for i in range(3)]
    lo = [w.local(I.wcat.at[at_rows(512 * c, 512, 512), pl.ds(1536, 512)], slot(0).at[at_rows(512 * c, 512, 512)]),
          w.local(I.wor, slot(0).at[at_rows(512 * (1 - c), 512, 512)])]
    do(sc.second, P3, -1); do(sc.third, P3, 2)
    ld.small.wait(); ld.resid.wait()
    r.gsum[...] = jnp.zeros((8, 1024), f32)
    gain = lambda i: r.small[i:i + 1, :]
    gdh.wait_recv()
    def back2(i, _):
        q = at_rows(i * 64, 64, 64); qo = at_rows(256 * c + i * 64, 64, 64)
        rs_ = r.resid[q, :]
        s2 = lax.rsqrt(jnp.mean(rs_ * rs_, axis=1, keepdims=True) + EPS)
        d = r.dho[q, :] + r.dhr[q, :]
        r.gsum[1:2, :] += jnp.sum(d * rs_ * s2, axis=0, keepdims=True)
        wt = d * gain(1)
        inner = jnp.mean(wt * rs_, axis=1, keepdims=True)
        dr = r.dffo[qo, :].astype(f32) + (s2 * wt - rs_ * (s2 * s2 * s2) * inner)
        r.resid[q, :] = dr
        r.h2[qo, :] = dr.astype(bf)
        return 0
    lax.fori_loop(0, 4, back2, 0)
    gdm = w.send(r.h2.at[own], r.h2.at[own], other)
    do(sc.first, P3, 0); do(sc.second, P3, 1); do(sc.third, P3, -1)
    for q in (ld.y, ld.ext, ld.conv, ld.bcx, ld.h, ld.tok, ld.keep): q.wait()
    for q in lo: q.wait()
    gdm.wait_recv()
    d_y = nt(r.h2[:, :512], slot(0)[0:512, :]) + nt(r.h2[:, 512:], slot(0)[512:1024, :])
    cpart = r.bcx[:, 512:1024].astype(f32)
    r.dcv[0:512, :] = d_y * cpart
    r.bcx[:, 512:1024] = (d_y * r.conv[...].astype(f32)).astype(bf)
    ghalo = w.send(r.dcv.at[pl.ds(0, 8)], r.dcv.at[pl.ds(512, 8)], prv)
    def d_out(i, _):
        t = tn(r.y[:, at_rows(256 * i, 256, 256)], r.h2[...]).astype(bf)
        for xx in range(4):
            for u in (0, 1):
                v = t[64 * xx + 32 * u:64 * xx + 32 * u + 32]
                r.up[at_rows(256 * i + 64 * xx + 32 * u, 32, 32), 0:512] = jnp.where(c == 0, v[:, 512:], v[:, :512])
                grads[1][2 * c + i, xx, u, 96:128, :] = jnp.where(c == 0, v[:, :512], v[:, 512:])
        return 0
    lax.fori_loop(0, 2, d_out, 0)
    gdo = [w.send(r.up.at[pl.ds(256 * i + 64 * xx + 32 * u, 32), pl.ds(0, 512)], grads[1].at[2 * c + i, xx, u, pl.ds(96, 32), :], other)
           for i in (0, 1) for xx in range(4) for u in (0, 1)]
    tap = [r.small[2 + i:3 + i, col(512 * c, 512)] for i in range(3)]
    for q in range(0, 512, 128):
        dv = r.dcv[q:q + 128, :]
        for i in range(3):
            r.gsum[2 + i:3 + i, col(512 * c, 512)] += jnp.sum(dv * r.ext[14 + i + q:142 + i + q, :], axis=0, keepdims=True)
    ghalo.wait_recv()
    r.dcv[512:520, :] = r.dcv[512:520, :] * (k < 31).astype(f32)
    for q in range(0, 512, 128):
        dx = tap[2] * r.dcv[q:q + 128, :] + tap[1] * r.dcv[q + 1:q + 129, :] + tap[0] * r.dcv[q + 2:q + 130, :]
        bp, xp = r.bcx[q:q + 128, 0:512].astype(f32), r.bcx[q:q + 128, 1024:1536].astype(f32)
        r.bcx[q:q + 128, 0:512] = (dx * xp).astype(bf)
        r.bcx[q:q + 128, 1024:1536] = (dx * bp).astype(bf)
    def d_in(yy, _):
        t = tn(r.h[:, at_rows(256 * yy, 256, 256)], r.bcx[...]).astype(bf)
        for p in range(3):
            for xx in range(4):
                for u in (0, 1): grads[1][yy, xx, u, 32 * p:32 * p + 32, :] = t[64 * xx + 32 * u:64 * xx + 32 * u + 32, 512 * p:512 * p + 512]
        return 0
    lax.fori_loop(0, 4, d_in, 0)
    for q in gdo: q.wait_recv()
    for j in JS: do(sc.first, P1, j)
    do(sc.second, P3, 0); do(sc.third, P3, 1)
    gdh.wait_send()
    for q in lin: q.wait()
    for rr, acc in ((oth, r.dhs), (own, r.dho)):
        acc[...] = sum(nt(r.bcx[rr, 512 * i:512 * i + 512], slot(i + 1)[...]) for i in range(3))
    gdh = w.send(r.dhs, r.dhr, other)
    la = w.local(I.act, r.gate)
    lw = [w.local(I.wd.at[at_rows(FH * c, FH, FH), :], W.at[c]), w.local(I.wdr.at[at_rows(FH * c, FH, FH), :], W.at[1 - c])]
    do(sc.first, P2, 2); do(sc.third, P3, 0); do(sc.second, P1, 2)
    gdh.wait_recv()
    def back1(i, _):
        q = at_rows(i * 64, 64, 64)
        t = r.tok[q, :].astype(f32)
        s1 = lax.rsqrt(jnp.mean(t * t, axis=1, keepdims=True) + EPS)
        d = r.dho[q, :] + r.dhr[q, :]
        r.gsum[0:1, :] += jnp.sum(d * t * s1, axis=0, keepdims=True)
        wt = d * gain(0)
        inner = jnp.mean(wt * t, axis=1, keepdims=True)
        r.dho[q, :] = r.resid[q, :] + (s1 * wt - t * (s1 * s1 * s1) * inner)
        return 0
    lax.fori_loop(0, 4, back1, 0)
    pl.semaphore_signal(free, inc=1, device_id=other, device_id_type=MESH)
    ltk = w.local(r.dho, O.dtok)
    eye = (lax.broadcasted_iota(jnp.int32, (8, 128), 0) == lax.broadcasted_iota(jnp.int32, (8, 128), 1)).astype(f32).astype(bf)
    sm = tn(r.gsum[...].astype(bf), eye).astype(bf)
    for yy in range(4):
        for xx in range(4):
            for u in (0, 1):
                o = 256 * yy + 64 * xx + 32 * u
                grads[0][yy, xx, u] = sm[o:o + 32]
    for j in JS: do(sc.first, P0, j)
    PS = P1 + P0
    do(sc.second, P1, -1); do(sc.last1, P3)
    do(sc.first, P2, -1); do(sc.second, P2, 2); do(sc.second, P1, 1); do(sc.third, P1, 2)
    for j in JS: do(sc.second, P0, j)
    do(sc.second, P1, 0); do(sc.third, P1, -1); do(sc.last2, P3)
    gdh.wait_send()
    la.wait()
    for q in lw: q.wait()
    ltk.wait()
    for rr, acc in ((oth, r.dhs), (own, r.dho)):
        for h_ in (0, 1): acc[:, 512 * h_:512 * h_ + 512] = dot(r.gate[rr, :], W[h_])
    pl.semaphore_wait(free, 1)
    gdh = w.send(r.dhs, r.dhr, other)
    do(sc.first, P2, 1); do(sc.second, P2, -1); do(sc.third, P2, 2); do(sc.third, P1, 1)
    for j in JS: do(sc.third, P0, j)
    do(sc.third, P1, 0)
    t3 = lambda n: [(0, 0, 256, O.dd, 512 * c + (0 if n is F.f3a else 256))]
    for n in P3: sc.last3(n, t3(n))
    do(sc.first, P2, 0); do(sc.second, P2, 1); do(sc.third, P2, -1); do(sc.last1, PS)
    gdh.wait_recv()
    lres = w.local(I.resid, r.resid)
    lres.wait()
    r.tok[...] = (r.keep[...] * (r.resid[...] + (r.dho[...] + r.dhr[...]))).astype(bf)
    lmx = w.local(r.tok, O.mixed)
    do(sc.second, P2, 0); do(sc.third, P2, 1); do(sc.last2, PS)
    do(sc.third, P2, 0)
    do(sc.last1, P2)
    for n, o in ((F.f1a, 0), (F.f1b, 256)):
        sc.last3(n, [(32 * p, 0, 256, O.din, 1024 * p + 512 * c + o) for p in range(3)] + [(96, 0, 256, O.dout, 512 * c + o)])
    sc.last3(F.f1s, [(0, 0, 128, O.ds.at[c], None)])
    do(sc.last2, P2)
    sc.last3(F.f2a, [(0, 0, FH, O.dg, FH * c)])
    sc.last3(F.f2b, [(0, 0, FH, O.du, FH * c)])
    for f in vars(F).values(): sc.wait_out(f)
    lmx.wait()
    w.drain()

def backward_all(a, tokens, keep):
    a = Box(a)
    a.ddown = a.ddown.reshape(2, 2, 4, 2, 144, 512)
    scr = [*B_SCR.values()] + GRADS + GRADS + [v for t in RFLOWS.values() for v in flow_scratch(t)]
    outs = call(backward_kernel, [*B_OUT.values()], scr, 2, 63, [pltpu.SemaphoreType.REGULAR], *vars(a).values(), tokens, keep)
    return Box(dict(zip(B_OUT, outs)))


def body(tokens, lengths, norm1_gain, in_proj, conv_weight, out_proj, norm2_gain, w_gate, w_up, w_down, cotangent):
    rows = tokens.shape[0]
    place = lax.axis_index("shard")
    slot = lax.axis_index("rep")
    slot_ids = jnp.arange(lengths.shape[0], dtype=jnp.int32)
    length = jnp.sum(jnp.where(slot_ids == slot, lengths, 0))
    valid = jnp.clip(length - place * rows, 0, rows)
    keep = (jnp.arange(rows, dtype=jnp.int32) < valid).astype(jnp.float32)[:, None]
    a = forward_all(tokens, cotangent, keep, in_proj, out_proj, smalls(norm1_gain, norm2_gain, conv_weight), w_gate, w_up, w_down)
    b = backward_all(a, tokens, keep)
    sm = b.ds[0] + b.ds[1]
    return b.mixed, b.dtok, sm[:, 0], b.din, sm[:, 2:5].T, b.dout, sm[:, 1], b.dg, b.du, b.dd

def solution(mesh):
    tok = P(("rep", "shard"), None)
    par = (P("shard"), P("shard", None), P(None, "shard"), P("shard", None), P("shard"), P("shard", None), P("shard", None), P("shard", None))
    return jax.shard_map(body, mesh=mesh, in_specs=(tok, P()) + par + (tok,), out_specs=(tok, tok) + par, check_vma=False)
```

time: 2020 us -> 291 us (0.14)
  waiting for transfers between devices: 1430 us -> 0 us
  blocking collectives: 429 us -> 0 us
  Pallas kernels: 0 us -> 274 us
  matrix products: 100 us -> 0 us
  other arithmetic: 27.5 us -> 3.43 us
    reduce_scatter x5 -> x0, waiting for transfers between devices: 959 us -> none  [the longest x1 335 us: body(): lax.psum_scatter(d_proj_out, 'shard', scatter_dimension=0, tiled=True)]
    unnamed x13 -> x0, waiting for transfers between devices: 327 us -> none
    unnamed x2 -> x0, blocking collectives: 327 us -> none
    pallas_call x0 -> x2, Pallas kernels: none -> 274 us  [call(): pl.pallas_call(kernel, out_shape=tuple((jax.ShapeDtypeStruct(*v) for v in...]
    all_gather x5 -> x0, waiting for transfers between devices: 104 us -> none  [the longest x1 78 us: body(): lax.all_gather(w_down, 'shard', axis=0, tiled=True)]
    dot_general x15 -> x0, matrix products: 100 us -> none  [the longest x5 38.8 us: weight_grad(): lax.dot_general(left, right, (((0,), (0,)), ((), ())), preferred_element_...]
    all_gather x1 -> x0, blocking collectives: 95.7 us -> none  [body(): lax.all_gather(conv_weight, 'shard', axis=1, tiled=True)]
    psum x1 -> x0, waiting for transfers between devices: 30.8 us -> none  [body(): lax.psum(shares[1].astype(jnp.bfloat16), 'rep').astype(jnp.float32)]
  transfers between devices with their start and end apart: 14 -> 0, of which waited for: 10 -> 0; matrix products, arithmetic and copies ran while one was open for 5% -> 0% of each run, Pallas kernels for 0% -> 0%
where the time goes in v2:
time: 291 us; the launch traced here: 290 us
  Pallas kernels  274 us (94%)
  local copies, waits for them, and re-layouts  11.4 us (4%)
  other arithmetic  3.43 us (1%)
    pallas_call x2, Pallas kernels, call(): pl.pallas_call(kernel, out_shape=tuple((jax.ShapeDtypeStruct(*v) for v in...  274 us
    unnamed x19, local copies, waits for them, and re-layouts  9.11 us

profile of v2, /device:TPU:1, one launch (start us, length us, event | category | flops | bytes accessed | tf_op | source)
XLA Modules:
  0.0 289.9 jit_solution(12721560218894438971)
XLA Ops:
  0.6 1.3 fusion.6
  2.6 0.7 copy.26
  3.3 0.8 copy.25
  4.1 0.7 copy.27
  4.9 0.7 fusion.5.refs_5_
  5.5 0.7 fusion.refs_2_.refs_18_
  6.2 123.7 %shard_map.186 = (bf16[1024,6784]{1,0:T(8,128)(2,1)}, bf16[4608,512]{1,0:T(8,128)(2,1)}, bf16[512,512]{1,0:T(8,128)(2,1)}, bf16[4608,512]{1,0:T(8,128)(2,1)}, bf...) custom-call(bf16[256,1024]{1,0:T(8,128)(2,1)} %refs_17_.1, ...), custom_call_target="tpu_custom_call" | custom-call | tf_op jit(solution)/shard_map/pallas_call | solution.py:339
  129.9 150.0 %shard_map.187 = (bf16[256,1024]{1,0:T(8,128)(2,1)}, f32[256,1024]{1,0:T(8,128)}, f32[16,3072]{1,0:T(8,128)}, f32[16,1024]{1,0:T(8,128)}, f32[16,4608]{1,0:T(8,1...) custom-call(bf16[1024,6784]{1,0:T(8,128)(2,1)} %get-tuple-element.35.refs_0_, ...), custom_call_target="tpu_custom_call" | custom-call | tf_op jit(solution)/shard_map/pallas_call | solution.py:339
  280.0 0.0 copy-start.3
  280.0 0.0 copy-start.4
  280.0 0.8 add_bitcast_fusion
  280.8 0.7 slice_reduce_fusion
  281.5 0.1 slice_bitcast_fusion
  281.6 0.7 copy.28
  282.3 1.9 copy.36
  284.2 2.3 copy.37
  286.5 0.0 copy-done.3
  286.5 0.7 copy.38
  287.2 0.0 copy-done.4
  287.2 0.6 copy.39
  287.8 0.7 copy.40
  288.5 0.7 copy.41
  289.2 0.0 copy-done
  289.2 0.7 copy.42
  (5 shorter events, 0.0 us)
Async XLA Ops:
  280.0 6.5 %copy-start.3 = (f32[16,3072]{1,0:T(8,128)S(1)}, f32[16,3072]{1,0:T(8,128)}, u32[]{:S(2)}) copy-start(f32[16,3072]{1,0:T(8,128)} %get-tuple-element.95) | copy-start | bytes 589828
  280.0 7.2 %copy-start.4 = (f32[16,1024]{1,0:T(8,128)S(1)}, f32[16,1024]{1,0:T(8,128)}, u32[]{:S(2)}) copy-start(f32[16,1024]{1,0:T(8,128)} %get-tuple-element.97) | copy-start | bytes 196612
  280.0 7.8 %copy-start.2 = (f32[16,4608]{1,0:T(8,128)S(1)}, f32[16,4608]{1,0:T(8,128)}, u32[]{:S(2)}) copy-start(f32[16,4608]{1,0:T(8,128)} %get-tuple-element.99) | copy-start | bytes 884740
  280.0 8.5 %copy-start.1 = (f32[16,4608]{1,0:T(8,128)S(1)}, f32[16,4608]{1,0:T(8,128)}, u32[]{:S(2)}) copy-start(f32[16,4608]{1,0:T(8,128)} %get-tuple-element.100) | copy-start | bytes 884740
  282.3 7.0 %copy-start = (f32[72,1024]{1,0:T(8,128)S(1)}, f32[72,1024]{1,0:T(8,128)}, u32[]{:S(2)}) copy-start(f32[72,1024]{1,0:T(8,128)} %get-tuple-element.101) | copy-start | bytes 884740
